TPU v7x, 256 devices: a whole 4x4x8 slice. The times are simulated.
256 devices in a mesh: ctx: 128 (over y, x, z), head: 2 (over core).
Axes of the slice: x: 4, y: 4, z: 8, core: 2. Of those that a mesh axis runs over, the one named last changes fastest.
Arguments:
- queries: bfloat16 [65536, 4, 4, 128], P('ctx', 'head')
- keys: bfloat16 [65536, 4, 128], P('ctx')
- values: bfloat16 [65536, 4, 128], P('ctx'), may hold values from -6 to 6
- output_gradient: bfloat16 [65536, 4, 4, 128], P('ctx', 'head'), may hold values from -6 to 6
- selected: int32 [128, 2], replicated, may hold values from 0 to 126, as said below
Outputs:
- attn_out: bfloat16 [65536, 4, 4, 128], P('ctx', 'head')
- grad_q: bfloat16 [65536, 4, 4, 128], P('ctx', 'head')
- grad_k: bfloat16 [65536, 4, 128], P('ctx', 'head')
- grad_v: bfloat16 [65536, 4, 128], P('ctx', 'head')
Inputs may be any that keep to these rules, and one draw needn't show every extreme that they name: selected[b, j] <= b for every block b; an entry equal to b selects no block; for b >= 2 the two entries of a row differ and both are below b.
All inputs are finite; a program needn't handle non-finite values.
Results may differ from a plain program's by a relative error of at most 0.011.
Values may be sent and summed in bfloat16 or wider, within the bound.
No kernel may reach another device: no remote copies, remote signals or barrier semaphores. Data moves between devices by JAX's collectives and lax.ppermute only.
A program may use at most 128 MiB of HBM per device.

v0:
```python
import functools
import math

import jax
import jax.numpy as jnp
from jax import lax
from jax.experimental import pallas as pl
from jax.experimental.pallas import tpu as pltpu
from jax.sharding import PartitionSpec as P

F32 = jnp.float32
BF16 = jnp.bfloat16
MIB = 1024 * 1024


def dot_nn(a, b):
    return lax.dot_general(a, b, (((1,), (0,)), ((), ())), preferred_element_type=F32)


def dot_nt(a, b):
    return lax.dot_general(a, b, (((1,), (1,)), ((), ())), preferred_element_type=F32)


def dot_tn(a, b):
    return lax.dot_general(a, b, (((0,), (0,)), ((), ())), preferred_element_type=F32)


def pick_kernel(picks, held, out):
    blocks, rows, _ = held.shape

    def body(step, _):
        for sub in range(8):
            at = step * 8 + sub
            for j in range(2):
                out[at, j * rows : (j + 1) * rows, :] = held[picks[at * 2 + j]]
        return 0

    lax.fori_loop(0, blocks // 8, body, 0)


def pick_pieces(held, picks):
    blocks, rows, width = held.shape
    return pl.pallas_call(
        pick_kernel,
        out_shape=jax.ShapeDtypeStruct((blocks, 2 * rows, width), held.dtype),
        in_specs=[
            pl.BlockSpec(memory_space=pltpu.SMEM),
            pl.BlockSpec(memory_space=pltpu.VMEM),
        ],
        out_specs=pl.BlockSpec(memory_space=pltpu.VMEM),
        name="pick_pieces",
    )(picks, held)


def collect_kernel(picks, arrived, out, total):
    blocks, rows2, _ = arrived.shape
    rows = rows2 // 2
    total[...] = jnp.zeros_like(total)

    def body(step, _):
        for sub in range(8):
            at = step * 8 + sub
            for j in range(2):
                owner = picks[at * 2 + j]
                total[owner] += arrived[at, j * rows : (j + 1) * rows, :].astype(F32)
        return 0

    lax.fori_loop(0, blocks // 8, body, 0)
    out[...] = total[...].astype(out.dtype)


def collect_pieces(arrived, picks):
    blocks, rows2, width = arrived.shape
    return pl.pallas_call(
        collect_kernel,
        out_shape=jax.ShapeDtypeStruct((blocks, rows2 // 2, width), arrived.dtype),
        in_specs=[
            pl.BlockSpec(memory_space=pltpu.SMEM),
            pl.BlockSpec(memory_space=pltpu.VMEM),
        ],
        out_specs=pl.BlockSpec(memory_space=pltpu.VMEM),
        scratch_shapes=[pltpu.VMEM((blocks, rows2 // 2, width), F32)],
        name="collect_pieces",
    )(picks, arrived)


def lower_triangle(rows):
    return lax.broadcasted_iota(jnp.int32, (rows, rows), 0) >= lax.broadcasted_iota(
        jnp.int32, (rows, rows), 1
    )


def own_forward_kernel(log_scale, q_ref, kv_ref, out_ref, lse_ref):
    half = q_ref.shape[2] // 2
    seen = lower_triangle(half)
    for tile in range(2):
        rows = slice(tile * half, (tile + 1) * half)
        query = q_ref[0, 0, rows, :]
        parts = []
        for col in range(tile + 1):
            cols = slice(col * half, (col + 1) * half)
            scores = dot_nt(query, kv_ref[0, 0, cols, :])
            if col == tile:
                scores = jnp.where(seen, scores, -jnp.inf)
            parts.append(scores)
        top = parts[0].max(axis=-1, keepdims=True)
        for scores in parts[1:]:
            top = jnp.maximum(top, scores.max(axis=-1, keepdims=True))
        top = top * log_scale
        weight, total = None, None
        for col, scores in enumerate(parts):
            cols = slice(col * half, (col + 1) * half)
            probs = jnp.exp2(scores * log_scale - top)
            summed = probs.sum(axis=-1, keepdims=True)
            product = dot_nn(probs.astype(BF16), kv_ref[0, 1, cols, :])
            weight = summed if weight is None else weight + summed
            total = product if total is None else total + product
        out_ref[0, 0, rows, :] = total * (1.0 / weight)
        lse_ref[0, 0, rows, :] = jnp.broadcast_to(top + jnp.log2(weight), total.shape)


def own_forward(queries, own_kv, softmax_scale):
    kv_count, groups, rows, width = queries.shape
    by_group = pl.BlockSpec((1, 1, rows, width), lambda n, g: (n, g, 0, 0))
    return pl.pallas_call(
        functools.partial(own_forward_kernel, softmax_scale * math.log2(math.e)),
        grid=(kv_count, groups),
        out_shape=(
            jax.ShapeDtypeStruct(queries.shape, F32),
            jax.ShapeDtypeStruct(queries.shape, F32),
        ),
        in_specs=[by_group, pl.BlockSpec((1, 2, rows, width), lambda n, g: (n, 0, 0, 0))],
        out_specs=(by_group, by_group),
        compiler_params=pltpu.CompilerParams(vmem_limit_bytes=24 * MIB),
        cost_estimate=pl.CostEstimate(
            flops=4 * kv_count * groups * rows * rows * width,
            bytes_accessed=12 * kv_count * groups * rows * width,
            transcendentals=kv_count * groups * rows * rows,
        ),
        name="own_forward",
    )(queries, own_kv)


def near_kernel(
    softmax_scale,
    tiles,
    seen_ref,
    q_ref,
    do_ref,
    near_ref,
    own_out_ref,
    own_lse_ref,
    out_ref,
    stat_ref,
    dq_ref,
    dnear_ref,
    dk_acc,
    dv_acc,
):
    log_scale = softmax_scale * math.log2(math.e)
    groups, _, piece, width = near_ref.shape[2:]
    rows = groups * piece
    step = pl.program_id(1)
    query = q_ref[0]
    grads = do_ref[0]
    keys = [near_ref[0, 0, :, j].reshape(rows, width) for j in range(2)]
    values = [near_ref[0, 1, :, j].reshape(rows, width) for j in range(2)]
    seen = [seen_ref[j] > 0 for j in range(2)]

    @pl.when(step == 0)
    def _():
        dk_acc[...] = jnp.zeros_like(dk_acc)
        dv_acc[...] = jnp.zeros_like(dv_acc)

    own_lse = own_lse_ref[0][:, :1]
    scores = [dot_nt(query, keys[j]) for j in range(2)]
    top = own_lse
    for j in range(2):
        peak = scores[j].max(axis=-1, keepdims=True) * log_scale
        top = jnp.maximum(top, jnp.where(seen[j], peak, -jnp.inf))
    own_share = jnp.exp2(own_lse - top)
    weight = own_share
    total = own_share * own_out_ref[0]
    probs, low = [], []
    for j in range(2):
        shift = jnp.where(seen[j], top, jnp.inf)
        probs.append(jnp.exp2(scores[j] * log_scale - shift))
        weight = weight + probs[j].sum(axis=-1, keepdims=True)
        low.append(probs[j].astype(BF16))
        total = total + dot_nn(low[j], values[j])
    inverse = 1.0 / weight
    head_out = (total * inverse).astype(BF16)
    out_ref[0] = head_out
    grads_f = grads.astype(F32)
    row_dot = jnp.sum(grads_f * head_out.astype(F32), axis=-1, keepdims=True)
    lane = lax.broadcasted_iota(jnp.int32, (query.shape[0], width), 1)
    stat_ref[0] = jnp.where(lane < width // 2, top + jnp.log2(weight), row_dot)
    grads_low = (grads_f * inverse).astype(BF16)
    shift_dot = row_dot * inverse
    dq = None
    for j in range(2):
        grad_probs = dot_nt(grads_low, values[j])
        grad_scores = (probs[j] * (grad_probs - shift_dot)).astype(BF16)
        term = dot_nn(grad_scores, keys[j])
        dq = term if dq is None else dq + term
        dk_acc[j] += dot_tn(grad_scores, query)
        dv_acc[j] += dot_tn(low[j], grads_low)
    dq_ref[0] = dq

    @pl.when(step == tiles - 1)
    def _():
        for j in range(2):
            dnear_ref[0, 0, :, j] = (
                (dk_acc[j] * softmax_scale).astype(BF16).reshape(groups, piece, width)
            )
            dnear_ref[0, 1, :, j] = dv_acc[j].astype(BF16).reshape(groups, piece, width)


def near_attention(seen, queries, grads, near, own_out, own_lse, softmax_scale, tile):
    kv_count, rows, width = queries.shape
    tiles = rows // tile
    _, _, groups, _, piece, _ = near.shape
    by_tile = pl.BlockSpec((1, tile, width), lambda n, i: (n, i, 0))
    by_head = pl.BlockSpec((1,) + near.shape[1:], lambda n, i: (n, 0, 0, 0, 0, 0))
    return pl.pallas_call(
        functools.partial(near_kernel, softmax_scale, tiles),
        grid=(kv_count, tiles),
        out_shape=(
            jax.ShapeDtypeStruct(queries.shape, BF16),
            jax.ShapeDtypeStruct(queries.shape, F32),
            jax.ShapeDtypeStruct(queries.shape, F32),
            jax.ShapeDtypeStruct(near.shape, BF16),
        ),
        in_specs=[
            pl.BlockSpec(memory_space=pltpu.SMEM),
            by_tile,
            by_tile,
            by_head,
            by_tile,
            by_tile,
        ],
        out_specs=(by_tile, by_tile, by_tile, by_head),
        scratch_shapes=[
            pltpu.VMEM((2, groups * piece, width), F32),
            pltpu.VMEM((2, groups * piece, width), F32),
        ],
        compiler_params=pltpu.CompilerParams(vmem_limit_bytes=40 * MIB),
        cost_estimate=pl.CostEstimate(
            flops=20 * kv_count * rows * groups * piece * width,
            bytes_accessed=20 * kv_count * rows * width,
            transcendentals=2 * kv_count * rows * groups * piece,
        ),
        name="near_attention",
    )(seen, queries, grads, near, own_out, own_lse)


def own_backward_kernel(
    softmax_scale, groups, q_ref, do_ref, kv_ref, stat_ref, dq_near_ref, dq_ref, dkv_ref
):
    log_scale = softmax_scale * math.log2(math.e)
    half = q_ref.shape[2] // 2
    width = q_ref.shape[3]
    step = pl.program_id(1)
    triangle = lower_triangle(half)

    @pl.when(step == 0)
    def _():
        dkv_ref[...] = jnp.zeros_like(dkv_ref)

    for tile in range(2):
        rows = slice(tile * half, (tile + 1) * half)
        query = q_ref[0, 0, rows, :]
        grads = do_ref[0, 0, rows, :]
        lse = stat_ref[0, 0, rows, :1]
        row_dot = stat_ref[0, 0, rows, width // 2 : width // 2 + 1]
        dq = dq_near_ref[0, 0, rows, :]
        for col in range(tile + 1):
            cols = slice(col * half, (col + 1) * half)
            keys = kv_ref[0, 0, cols, :]
            probs = jnp.exp2(dot_nt(query, keys) * log_scale - lse)
            if col == tile:
                probs = jnp.where(triangle, probs, 0.0)
            grad_probs = dot_nt(grads, kv_ref[0, 1, cols, :])
            grad_scores = (probs * (grad_probs - row_dot)).astype(BF16)
            dq = dq + dot_nn(grad_scores, keys)
            dkv_ref[0, 0, cols, :] += dot_tn(grad_scores, query)
            dkv_ref[0, 1, cols, :] += dot_tn(probs.astype(BF16), grads)
        dq_ref[0, 0, rows, :] = (dq * softmax_scale).astype(BF16)

    @pl.when(step == groups - 1)
    def _():
        dkv_ref[0, 0] = dkv_ref[0, 0] * softmax_scale


def own_backward(queries, grads, own_kv, stat, dq_near, softmax_scale):
    kv_count, groups, rows, width = queries.shape
    by_group = pl.BlockSpec((1, 1, rows, width), lambda n, g: (n, g, 0, 0))
    by_head = pl.BlockSpec((1, 2, rows, width), lambda n, g: (n, 0, 0, 0))
    return pl.pallas_call(
        functools.partial(own_backward_kernel, softmax_scale, groups),
        grid=(kv_count, groups),
        out_shape=(
            jax.ShapeDtypeStruct(queries.shape, BF16),
            jax.ShapeDtypeStruct(own_kv.shape, F32),
        ),
        in_specs=[by_group, by_group, by_head, by_group, by_group],
        out_specs=(by_group, by_head),
        compiler_params=pltpu.CompilerParams(vmem_limit_bytes=24 * MIB),
        cost_estimate=pl.CostEstimate(
            flops=10 * kv_count * groups * rows * rows * width,
            bytes_accessed=16 * kv_count * groups * rows * width,
            transcendentals=kv_count * groups * rows * rows,
        ),
        name="own_backward",
    )(queries, grads, own_kv, stat, dq_near)


def exchange(pieces):
    return lax.ppermute(pieces, "head", [(0, 1), (1, 0)])


def spread(pieces):
    return lax.all_to_all(pieces, "ctx", split_axis=0, concat_axis=0, tiled=True)


def on_device(queries, keys, values, output_gradient, selected):
    rows_block, own_groups, kv_count, width = queries.shape
    blocks = lax.axis_size("ctx")
    own_index = lax.axis_index("ctx")
    core = lax.axis_index("head")
    half_kv = kv_count // 2
    mine, theirs = core * half_kv, (1 - core) * half_kv
    softmax_scale = width ** (-0.5)
    piece_groups = blocks // (2 * half_kv)
    piece = rows_block // piece_groups
    picks = selected.reshape(-1)
    own_picks = lax.dynamic_index_in_dim(selected, own_index, 0, keepdims=False)
    seen = (own_picks < own_index).astype(jnp.int32)

    both = jnp.stack([keys, values], axis=0)
    both = lax.dynamic_slice_in_dim(both, mine, half_kv, axis=2)
    own_kv = jnp.transpose(both, (2, 0, 1, 3))
    held = spread(own_kv.reshape(blocks, piece, width))

    inputs = jnp.transpose(jnp.stack([queries, output_gradient], axis=0), (0, 3, 2, 1, 4))
    kept = lax.dynamic_slice_in_dim(inputs, mine, half_kv, axis=1)
    fetched = exchange(lax.dynamic_slice_in_dim(inputs, theirs, half_kv, axis=1))
    inputs = jnp.concatenate([kept, fetched], axis=2)
    q_all, do_all = inputs[0], inputs[1]
    own_out, own_lse = own_forward(q_all, own_kv, softmax_scale)

    near = spread(pick_pieces(held, picks))
    near = near.reshape(half_kv, 2, piece_groups, 2, piece, width)
    flat = (half_kv, 2 * own_groups * rows_block, width)
    attn, stat, dq_near, dnear = near_attention(
        seen,
        q_all.reshape(flat),
        do_all.reshape(flat),
        near,
        own_out.reshape(flat),
        own_lse.reshape(flat),
        softmax_scale,
        rows_block,
    )
    arrived = spread(dnear.reshape(blocks, 2 * piece, width))
    dq, dkv = own_backward(
        q_all, do_all, own_kv, stat.reshape(q_all.shape), dq_near.reshape(q_all.shape), softmax_scale
    )
    home = spread(collect_pieces(arrived, picks))

    def give_back(result):
        result = result.reshape(half_kv, 2 * own_groups, rows_block, width)
        back = exchange(result[:, own_groups:])
        whole = jnp.zeros((kv_count,) + back.shape[1:], result.dtype)
        whole = lax.dynamic_update_slice_in_dim(whole, result[:, :own_groups], mine, 0)
        whole = lax.dynamic_update_slice_in_dim(whole, back, theirs, 0)
        return jnp.transpose(whole, (2, 1, 0, 3))

    attn_out = give_back(attn)
    grad_q = give_back(dq)
    grads = (home.reshape(own_kv.shape).astype(F32) + dkv).astype(BF16)
    grad_k, grad_v = (jnp.transpose(grads[:, part], (1, 0, 2)) for part in range(2))
    return (attn_out, grad_q, grad_k, grad_v)


def solution(mesh):
    return jax.shard_map(
        on_device,
        mesh=mesh,
        in_specs=(
            P("ctx", "head", None, None),
            P("ctx", None, None),
            P("ctx", None, None),
            P("ctx", "head", None, None),
            P(),
        ),
        out_specs=(
            P("ctx", "head", None, None),
            P("ctx", "head", None, None),
            P("ctx", "head", None),
            P("ctx", "head", None),
        ),
        check_vma=False,
    )
```

profile of v0, /device:TPU:32, one launch (start us, length us, event | category | flops | bytes accessed | tf_op | source)
XLA Modules:
  0.0 173.8 jit_solution(12542743949597488785)
XLA Ops:
  0.6 1.3 copy_bitcast_fusion.2
  2.8 15.0 %all-to-all-start = ((bf16[128,16,128]{2,1,0:T(8,128)(2,1)}), bf16[128,16,128]{2,1,0:T(8,128)(2,1)S(1)}, u32[]{:S(2)}, u32[]{:S(2)}) async-start(bf16[128,16,128]{2,1,0:T(8,128)(2,1)} %bitcast.9), calls=%async_computation | async-start | bytes 1048576 | tf_op jit(solution)/shard_map/all_to_all | solution.py:323
  18.7 19.3 %all-to-all-done.held = bf16[128,16,128]{2,1,0:T(8,128)(2,1)S(1)} async-done(((bf16[128,16,128]{2,1,0:T(8,128)(2,1)}), bf16[128,16,128]{2,1,0:T(8,128)(2,1)S(1)}, u32[]{:S(2)}, u32[]{:S(2)}) %all-to-all-start) | async-done | bytes 524320 | tf_op jit(solution)/shard_map/all_to_all | solution.py:323
  38.8 2.4 %pick_pieces.1 = bf16[128,32,128]{2,1,0:T(8,128)(2,1)} custom-call(s32[256]{0:T(256)} %reshape.42.picks, bf16[128,16,128]{2,1,0:T(8,128)(2,1)} %copy-done.14), custom_call_target="tpu_custom_call" | custom-call | tf_op jit(solution)/shard_map/pick_pieces/pallas_call | solution.py:43
  41.1 6.6 %all-to-all-start.1 = ((bf16[128,32,128]{2,1,0:T(8,128)(2,1)}), bf16[128,32,128]{2,1,0:T(8,128)(2,1)S(1)}, u32[]{:S(2)}, u32[]{:S(2)}) async-start(bf16[128,32,128]{2,1,0:T(8,128)(2,1)} %pick_pieces.1), calls=%async_computation.1 | async-start | bytes 2097152 | tf_op jit(solution)/shard_map/all_to_all | solution.py:323
  47.8 1.6 copy_bitcast_fusion
  50.8 2.5 %collective-permute-done = bf16[2,2,2,512,128]{4,3,2,1,0:T(8,128)(2,1)} collective-permute-done((bf16[2,2,2,512,128]{4,3,2,1,0:T(8,128)(2,1)S(1)}, bf16[2,2,2,512,128]{4,3,2,1,0:T(8,128)(2,1)}, u32[]{:S(2)}, u32[]{:S(2)}) %collective-permute-start) | collective-permute-done | bytes 1048608 | tf_op jit(solution)/shard_map/ppermute | solution.py:319
  53.4 1.4 pad_maximum_fusion
  54.8 6.2 %own_forward.1 = (f32[2,4,512,128]{3,2,1,0:T(8,128)S(1)}, f32[2,4,512,128]{3,2,1,0:T(8,128)S(1)}) custom-call(bf16[2,4,512,128]{3,2,1,0:T(8,128)(2,1)S(1)} %bitcast.43, bf16[2,2,512,128]{3,2,1,0:T(8,128)(2,1)S(1)} %fusion.10.kv_ref), custom_call_target="tpu_custom_call" | custom-call | flops 1073741824 | bytes 6291456 | tf_op jit(solution)/shard_map/own_forward/pallas_call | solution.py:125
  61.0 1.3 copy-done.9
  63.7 14.2 %all-to-all-done.1 = bf16[128,32,128]{2,1,0:T(8,128)(2,1)S(1)} async-done(((bf16[128,32,128]{2,1,0:T(8,128)(2,1)}), bf16[128,32,128]{2,1,0:T(8,128)(2,1)S(1)}, u32[]{:S(2)}, u32[]{:S(2)}) %all-to-all-start.1) | async-done | bytes 1048608 | tf_op jit(solution)/shard_map/all_to_all | solution.py:323
  79.1 1.6 copy-done.10
  80.7 1.6 copy-done.12
  82.3 25.6 %near_attention.1 = (bf16[2,2048,128]{2,1,0:T(8,128)(2,1)S(1)}, f32[2,2048,128]{2,1,0:T(8,128)S(1)}, f32[2,2048,128]{2,1,0:T(8,128)S(1)}, bf16[2,2,32,2,16,128]{5,4,3,2,1,0:T(8,128)(2,1)}) custom-call(s32[2]{0:T(128)S(1)} %fusion.7.seen_ref, bf16[2,2048,128]{2,1,0:T(8,128)(2,1)S(1)} %bitcast.44, bf16[2,2048,128]{2,1,0:T(8,128)(2,1)S(1)} %bitcast.41, ...), custom_call_target="tpu_custom_call" | custom-call | flops 5368709120 | bytes 10485760 | tf_op jit(solution)/shard_map/near_attention/pallas_call | solution.py:225
  107.9 1.4 copy-done.5
  110.6 7.7 %all-to-all-start.2 = ((bf16[128,32,128]{2,1,0:T(8,128)(2,1)}), bf16[128,32,128]{2,1,0:T(8,128)(2,1)}, u32[]{:S(2)}, u32[]{:S(2)}) async-start(bf16[128,32,128]{2,1,0:T(8,128)(2,1)} %bitcast.20), calls=%async_computation.2 | async-start | bytes 2097152 | tf_op jit(solution)/shard_map/all_to_all | solution.py:323
  120.5 1.6 copy-done.6
  122.1 1.6 copy-done.8
  123.7 9.8 %own_backward.1 = (bf16[2,4,512,128]{3,2,1,0:T(8,128)(2,1)S(1)}, f32[2,2,512,128]{3,2,1,0:T(8,128)S(1)}) custom-call(bf16[2,4,512,128]{3,2,1,0:T(8,128)(2,1)S(1)} %bitcast.45, bf16[2,4,512,128]{3,2,1,0:T(8,128)(2,1)S(1)} %bitcast.42, bf16[2,2,512,128]{3,2,1,0:T(8,128)(2,1)S(1)} %copy-done.4, f32[2,4,512,128]{3,2,1,0:T(8,128)S(1)} %bitcast.46, ...), custom_call_target="tpu_custom_call" | custom-call | flops 2684354560 | bytes 8388608 | tf_op jit(solution)/shard_map/own_backward/pallas_call | solution.py:299
  133.5 12.5 %all-to-all-done.2.arrived = bf16[128,32,128]{2,1,0:T(8,128)(2,1)} async-done(((bf16[128,32,128]{2,1,0:T(8,128)(2,1)}), bf16[128,32,128]{2,1,0:T(8,128)(2,1)}, u32[]{:S(2)}, u32[]{:S(2)}) %all-to-all-start.2) | async-done | bytes 1048608 | tf_op jit(solution)/shard_map/all_to_all | solution.py:323
  146.1 3.1 %collect_pieces.1 = bf16[128,16,128]{2,1,0:T(8,128)(2,1)} custom-call(s32[256]{0:T(256)} %reshape.42.picks, bf16[128,32,128]{2,1,0:T(8,128)(2,1)} %all-to-all-done.2.arrived), custom_call_target="tpu_custom_call" | custom-call | tf_op jit(solution)/shard_map/collect_pieces/pallas_call | solution.py:74
  149.1 6.6 %all-to-all-start.3 = ((bf16[128,16,128]{2,1,0:T(8,128)(2,1)}), bf16[128,16,128]{2,1,0:T(8,128)(2,1)S(1)}, u32[]{:S(2)}, u32[]{:S(2)}) async-start(bf16[128,16,128]{2,1,0:T(8,128)(2,1)} %collect_pieces.1), calls=%async_computation.3 | async-start | bytes 1048576 | tf_op jit(solution)/shard_map/all_to_all | solution.py:323
  159.7 1.8 %constant_dynamic-update-slice_fusion = bf16[4,2,512,128]{3,0,1,2:T(4,128)(2,1)S(1)} fusion(bf16[4,2,512,128]{3,0,1,2:T(4,128)(2,1)S(1)} %copy_dynamic-update-slice_fusion, bf16[2,2,512,128]{3,0,1,2:T(2,128)(2,1)} %collective-permute-done.1, s32[]{:T(128)S(6)} %select_n.17), kind=kLoop, calls=%fused_computation.26 | loop fusion | bytes 1048580 | tf_op jit(solution)/shard_map/dynamic_update_slice | solution.py:376
  162.9 8.8 %all-to-all-done.3 = bf16[128,16,128]{2,1,0:T(8,128)(2,1)S(1)} async-done(((bf16[128,16,128]{2,1,0:T(8,128)(2,1)}), bf16[128,16,128]{2,1,0:T(8,128)(2,1)S(1)}, u32[]{:S(2)}, u32[]{:S(2)}) %all-to-all-start.3) | async-done | bytes 524320 | tf_op jit(solution)/shard_map/all_to_all | solution.py:323
  (55 shorter events, 17.4 us)
Async XLA Ops:
  0.6 17.2 %copy-start.18 = (s32[128,2]{0,1:T(2,128)S(1)}, s32[128,2]{0,1:T(2,128)}, u32[]{:S(2)}) copy-start(s32[128,2]{0,1:T(2,128)} %param.9) | copy-start | bytes 3076
  2.8 35.1 %all-to-all-start = ((bf16[128,16,128]{2,1,0:T(8,128)(2,1)}), bf16[128,16,128]{2,1,0:T(8,128)(2,1)S(1)}, u32[]{:S(2)}, u32[]{:S(2)}) async-start(bf16[128,16,128]{2,1,0:T(8,128)(2,1)} %bitcast.9), calls=%async_computation | async-start | bytes 1048576 | tf_op jit(solution)/shard_map/all_to_all | solution.py:323
  17.9 29.9 %copy-start.17 = (bf16[512,2,4,128]{3,2,1,0:T(4,128)(2,1)S(1)}, bf16[512,2,4,128]{3,2,1,0:T(4,128)(2,1)}, u32[]{:S(2)}) copy-start(bf16[512,2,4,128]{3,2,1,0:T(4,128)(2,1)} %param.8) | copy-start | bytes 3145732
  41.1 36.7 %all-to-all-start.1 = ((bf16[128,32,128]{2,1,0:T(8,128)(2,1)}), bf16[128,32,128]{2,1,0:T(8,128)(2,1)S(1)}, u32[]{:S(2)}, u32[]{:S(2)}) async-start(bf16[128,32,128]{2,1,0:T(8,128)(2,1)} %pick_pieces.1), calls=%async_computation.1 | async-start | bytes 2097152 | tf_op jit(solution)/shard_map/all_to_all | solution.py:323
  50.6 2.8 %collective-permute-start = (bf16[2,2,2,512,128]{4,3,2,1,0:T(8,128)(2,1)S(1)}, bf16[2,2,2,512,128]{4,3,2,1,0:T(8,128)(2,1)}, u32[]{:S(2)}, u32[]{:S(2)}) collective-permute-start(bf16[2,2,2,512,128]{4,3,2,1,0:T(8,128)(2,1)S(1)} %get-tuple-element.30), channel_id=1, source_target_pairs={{0,1},{1,0},{2,3},{3,2},{4,5},{5,4},{6,7},{7,6},{8,9},{9,8},{10,11... | collective-permute-start | bytes 3145736 | tf_op jit(solution)/shard_map/ppermute | solution.py:319
  50.6 2.8 %copy-start.13 = (bf16[2,2,2,512,128]{4,3,2,1,0:T(8,128)(2,1)S(1)}, bf16[2,2,2,512,128]{4,3,2,1,0:T(8,128)(2,1)}, u32[]{:S(2)}) copy-start(bf16[2,2,2,512,128]{4,3,2,1,0:T(8,128)(2,1)} %get-tuple-element.31) | copy-start | bytes 3145732
  50.8 3.9 %copy-start.3 = (bf16[2,2,512,128]{3,2,1,0:T(8,128)(2,1)}, bf16[2,2,512,128]{3,2,1,0:T(8,128)(2,1)S(1)}, u32[]{:S(2)}) copy-start(bf16[2,2,512,128]{3,2,1,0:T(8,128)(2,1)S(1)} %fusion.10.kv_ref) | copy-start | bytes 1572868
  54.8 23.1 %copy-start = (bf16[1,2,4,512,128]{4,3,2,1,0:T(8,128)(2,1)}, bf16[1,2,4,512,128]{4,3,2,1,0:T(8,128)(2,1)S(1)}, u32[]{:S(2)}) copy-start(bf16[1,2,4,512,128]{4,3,2,1,0:T(8,128)(2,1)S(1)} %get-tuple-element.29) | copy-start | bytes 3145732
  61.0 1.4 copy-start.9
  62.4 1.3 copy-start.11
  79.1 1.6 copy-start.10
  80.7 1.6 copy-start.12
  107.9 1.4 copy-start.5
  109.2 1.3 copy-start.7
  110.6 35.5 %all-to-all-start.2 = ((bf16[128,32,128]{2,1,0:T(8,128)(2,1)}), bf16[128,32,128]{2,1,0:T(8,128)(2,1)}, u32[]{:S(2)}, u32[]{:S(2)}) async-start(bf16[128,32,128]{2,1,0:T(8,128)(2,1)} %bitcast.20), calls=%async_computation.2 | async-start | bytes 2097152 | tf_op jit(solution)/shard_map/all_to_all | solution.py:323
  118.3 2.2 %copy-start.2 = (bf16[1,2,4,512,128]{4,3,2,1,0:T(8,128)(2,1)S(1)}, bf16[1,2,4,512,128]{4,3,2,1,0:T(8,128)(2,1)}, u32[]{:S(2)}) copy-start(bf16[1,2,4,512,128]{4,3,2,1,0:T(8,128)(2,1)} %copy-done) | copy-start | bytes 3145732
  118.3 2.2 %copy-start.4 = (bf16[2,2,512,128]{3,2,1,0:T(8,128)(2,1)S(1)}, bf16[2,2,512,128]{3,2,1,0:T(8,128)(2,1)}, u32[]{:S(2)}) copy-start(bf16[2,2,512,128]{3,2,1,0:T(8,128)(2,1)} %copy-done.3) | copy-start | bytes 1572868
  120.5 39.2 %collective-permute-start.1 = (bf16[2,2,512,128]{3,0,1,2:T(2,128)(2,1)}, bf16[2,2,512,128]{3,0,1,2:T(2,128)(2,1)}, u32[]{:S(2)}, u32[]{:S(2)}) collective-permute-start(bf16[2,2,512,128]{3,0,1,2:T(2,128)(2,1)} %copy.31), channel_id=1, source_target_pairs={{0,1},{1,0},{2,3},{3,2},{4,5},{5,4},{6,7},{7,6},{8,9},{9,8},{10,11... | collective-permute-start | bytes 1572872 | tf_op jit(solution)/shard_map/ppermute | solution.py:319
  120.5 1.6 copy-start.6
  122.1 1.6 copy-start.8
  149.1 22.6 %all-to-all-start.3 = ((bf16[128,16,128]{2,1,0:T(8,128)(2,1)}), bf16[128,16,128]{2,1,0:T(8,128)(2,1)S(1)}, u32[]{:S(2)}, u32[]{:S(2)}) async-start(bf16[128,16,128]{2,1,0:T(8,128)(2,1)} %collect_pieces.1), calls=%async_computation.3 | async-start | bytes 1048576 | tf_op jit(solution)/shard_map/all_to_all | solution.py:323
  155.8 3.0 %copy-start.15 = (bf16[2,2,512,128]{3,2,1,0:T(8,128)(2,1)S(1)}, bf16[2,2,512,128]{3,2,1,0:T(8,128)(2,1)}, u32[]{:S(2)}) copy-start(bf16[2,2,512,128]{3,2,1,0:T(8,128)(2,1)} %get-tuple-element.35) | copy-start | bytes 1572868
  155.9 5.7 %collective-permute-start.2 = (bf16[2,2,512,128]{3,2,1,0:T(8,128)(2,1)S(1)}, bf16[2,2,512,128]{3,2,1,0:T(8,128)(2,1)S(1)}, u32[]{:S(2)}, u32[]{:S(2)}) collective-permute-start(bf16[2,2,512,128]{3,2,1,0:T(8,128)(2,1)S(1)} %get-tuple-element.32), channel_id=1, source_target_pairs={{0,1},{1,0},{2,3},{3,2},{4,5},{5,4},{6,7},{7,6},{8,9},{9,8},{10,11... | collective-permute-start | bytes 1572872 | tf_op jit(solution)/shard_map/ppermute | solution.py:319
  161.5 10.4 %copy-start.16 = (bf16[4,2,512,128]{3,0,1,2:T(4,128)(2,1)}, bf16[4,2,512,128]{3,0,1,2:T(4,128)(2,1)S(1)}, u32[]{:S(2)}) copy-start(bf16[4,2,512,128]{3,0,1,2:T(4,128)(2,1)S(1)} %constant_dynamic-update-slice_fusion) | copy-start | bytes 3145732
  (2 other events, 2.0 us)
where the time goes:
time: 175 us; the launch traced here: 174 us
  waiting for transfers between devices  57.4 us (33%)
  Pallas kernels  47.1 us (27%)
  starting transfers between devices  36.1 us (21%)
  local copies, waits for them, and re-layouts  28.7 us (16%)
  other arithmetic  3.74 us (2%)
    all_to_all x4, waiting for transfers between devices, spread(): lax.all_to_all(pieces, 'ctx', split_axis=0, concat_axis=0, tiled=True)  54.8 us
    all_to_all x4, starting transfers between devices, spread(): lax.all_to_all(pieces, 'ctx', split_axis=0, concat_axis=0, tiled=True)  36 us
    pallas_call x1, Pallas kernels, near_attention(): pl.pallas_call(functools.partial(near_kernel, softmax_scale, tiles), grid...  25.6 us
    unnamed x42, local copies, waits for them, and re-layouts  17.2 us
    pallas_call x1, Pallas kernels, own_backward(): pl.pallas_call(functools.partial(own_backward_kernel, softmax_scale, grou...  9.81 us
    pallas_call x1, Pallas kernels, own_forward(): pl.pallas_call(functools.partial(own_forward_kernel, softmax_scale * math...  6.22 us
  transfers between devices with their start and end apart: 7, of which 5 were waited for; matrix products, arithmetic and copies ran while one was open for 8% of the time, Pallas kernels for 11%

commit v1 on v0

v1 whole, which is shorter than its diff:
```python
import functools
import math

import jax
import jax.numpy as jnp
from jax import lax
from jax.experimental import pallas as pl
from jax.experimental.pallas import tpu as pltpu
from jax.sharding import PartitionSpec as P

F32 = jnp.float32
BF16 = jnp.bfloat16
GRANT = 60 * 1024 * 1024
SMALL_GRANT = 8 * 1024 * 1024


def dot_nn(a, b):
    return lax.dot_general(a, b, (((1,), (0,)), ((), ())), preferred_element_type=F32)


def dot_nt(a, b):
    return lax.dot_general(a, b, (((1,), (1,)), ((), ())), preferred_element_type=F32)


def dot_tn(a, b):
    return lax.dot_general(a, b, (((0,), (0,)), ((), ())), preferred_element_type=F32)


def pick_kernel(picks, held, out):
    count, rows2, _ = out.shape
    rows = rows2 // 2
    first = pl.program_id(0) * count

    def body(step, _):
        for sub in range(8):
            at = step * 8 + sub
            for j in range(2):
                out[at, j * rows : (j + 1) * rows, :] = held[picks[(first + at) * 2 + j]]
        return 0

    lax.fori_loop(0, count // 8, body, 0)


def pick_pieces(held, picks):
    blocks, rows, width = held.shape
    steps = 2 if blocks % 16 == 0 else 1
    return pl.pallas_call(
        pick_kernel,
        grid=(steps,),
        out_shape=jax.ShapeDtypeStruct((blocks, 2 * rows, width), held.dtype),
        in_specs=[
            pl.BlockSpec(memory_space=pltpu.SMEM),
            pl.BlockSpec((blocks, rows, width), lambda i: (0, 0, 0)),
        ],
        out_specs=pl.BlockSpec((blocks // steps, 2 * rows, width), lambda i: (i, 0, 0)),
        compiler_params=pltpu.CompilerParams(vmem_limit_bytes=SMALL_GRANT),
        name="pick_pieces",
    )(picks, held)


def collect_kernel(picks, arrived, out, total):
    count, rows2, _ = arrived.shape
    rows = rows2 // 2
    part = pl.program_id(0)

    @pl.when(part == 0)
    def _():
        total[...] = jnp.zeros_like(total)

    def body(step, _):
        for sub in range(8):
            at = step * 8 + sub
            for j in range(2):
                owner = picks[(part * count + at) * 2 + j]
                total[j, owner] += arrived[at, j * rows : (j + 1) * rows, :].astype(F32)
        return 0

    lax.fori_loop(0, count // 8, body, 0)

    @pl.when(part == pl.num_programs(0) - 1)
    def _():
        out[...] = (total[0] + total[1]).astype(out.dtype)


def collect_pieces(arrived, picks):
    blocks, rows2, width = arrived.shape
    steps = 2 if blocks % 16 == 0 else 1
    return pl.pallas_call(
        collect_kernel,
        grid=(steps,),
        out_shape=jax.ShapeDtypeStruct((blocks, rows2 // 2, width), arrived.dtype),
        in_specs=[
            pl.BlockSpec(memory_space=pltpu.SMEM),
            pl.BlockSpec((blocks // steps, rows2, width), lambda i: (i, 0, 0)),
        ],
        out_specs=pl.BlockSpec((blocks, rows2 // 2, width), lambda i: (0, 0, 0)),
        scratch_shapes=[pltpu.VMEM((2, blocks, rows2 // 2, width), F32)],
        compiler_params=pltpu.CompilerParams(vmem_limit_bytes=SMALL_GRANT),
        name="collect_pieces",
    )(picks, arrived)


def causal_pairs(rows):
    return lax.broadcasted_iota(jnp.int32, (rows, rows), 0) <= lax.broadcasted_iota(
        jnp.int32, (rows, rows), 1
    )


def own_forward_kernel(log_scale, q_ref, do_ref, kv_ref, qt_ref, dot_ref, out_ref, lse_ref, vt):
    width = kv_ref.shape[3]
    half = kv_ref.shape[2] // 2
    seen = causal_pairs(half)

    @pl.when(pl.program_id(1) == 0)
    def _():
        vt[...] = kv_ref[0, 1].T

    qt_ref[0] = q_ref[0, 0].T
    dot_ref[0] = do_ref[0, 0].T
    for tile in range(2):
        span = slice(tile * half, (tile + 1) * half)
        query = qt_ref[0, :, span]
        parts = []
        for col in range(tile + 1):
            scores = dot_nn(kv_ref[0, 0, col * half : (col + 1) * half, :], query)
            if col == tile:
                scores = jnp.where(seen, scores, -jnp.inf)
            parts.append(scores)
        top = parts[0].max(axis=0, keepdims=True)
        for scores in parts[1:]:
            top = jnp.maximum(top, scores.max(axis=0, keepdims=True))
        top = top * log_scale
        weight = jnp.zeros_like(top)
        total = jnp.zeros((width, half), F32)
        for col, scores in enumerate(parts):
            probs = jnp.exp2(scores * log_scale - top)
            weight = weight + probs.sum(axis=0, keepdims=True)
            total = total + dot_nn(vt[:, col * half : (col + 1) * half], probs.astype(BF16))
        out_ref[0, :, span] = total * (1.0 / weight)
        lse_ref[0, :, span] = jnp.broadcast_to(top + jnp.log2(weight), (8, half))


def own_forward(queries, grads, own_kv, softmax_scale):
    kv_count, groups, rows, width = queries.shape
    by_group = pl.BlockSpec((1, 1, rows, width), lambda n, g: (n, g, 0, 0))
    turned = pl.BlockSpec((1, width, rows), lambda n, g: (n, 0, g))
    return pl.pallas_call(
        functools.partial(own_forward_kernel, softmax_scale * math.log2(math.e)),
        grid=(kv_count, groups),
        out_shape=(
            jax.ShapeDtypeStruct((kv_count, width, groups * rows), BF16),
            jax.ShapeDtypeStruct((kv_count, width, groups * rows), BF16),
            jax.ShapeDtypeStruct((kv_count, width, groups * rows), F32),
            jax.ShapeDtypeStruct((kv_count, 8, groups * rows), F32),
        ),
        in_specs=[
            by_group,
            by_group,
            pl.BlockSpec((1, 2, rows, width), lambda n, g: (n, 0, 0, 0)),
        ],
        out_specs=(turned, turned, turned, pl.BlockSpec((1, 8, rows), lambda n, g: (n, 0, g))),
        scratch_shapes=[pltpu.VMEM((width, rows), BF16)],
        compiler_params=pltpu.CompilerParams(vmem_limit_bytes=GRANT),
        cost_estimate=pl.CostEstimate(
            flops=4 * kv_count * groups * rows * rows * width,
            bytes_accessed=12 * kv_count * groups * rows * width,
            transcendentals=kv_count * groups * rows * rows,
        ),
        name="own_forward",
    )(queries, grads, own_kv)


def near_kernel(
    softmax_scale,
    tiles,
    seen_ref,
    q_ref,
    qt_ref,
    dot_ref,
    near_ref,
    own_out_ref,
    own_lse_ref,
    out_ref,
    lse_ref,
    row_dot_ref,
    dq_ref,
    dnear_ref,
    dk_acc,
    dv_acc,
    kt,
    vt,
):
    log_scale = softmax_scale * math.log2(math.e)
    groups, _, piece, width = near_ref.shape[2:]
    rows = groups * piece
    step = pl.program_id(1)
    keys = [near_ref[0, 0, :, j].reshape(rows, width) for j in range(2)]
    values = [near_ref[0, 1, :, j].reshape(rows, width) for j in range(2)]
    seen = [seen_ref[j] > 0 for j in range(2)]

    @pl.when(step == 0)
    def _():
        dk_acc[...] = jnp.zeros_like(dk_acc)
        dv_acc[...] = jnp.zeros_like(dv_acc)
        for j in range(2):
            kt[j] = keys[j].T
            vt[j] = values[j].T

    query = qt_ref[0]
    own_lse = own_lse_ref[0, :1]
    scores = [dot_nn(keys[j], query) for j in range(2)]
    top = own_lse
    for j in range(2):
        peak = scores[j].max(axis=0, keepdims=True) * log_scale
        top = jnp.maximum(top, jnp.where(seen[j], peak, -jnp.inf))
    own_share = jnp.exp2(own_lse - top)
    weight = own_share
    total = own_share * own_out_ref[0]
    probs, low = [], []
    for j in range(2):
        shift = jnp.where(seen[j], top, jnp.inf)
        probs.append(jnp.exp2(scores[j] * log_scale - shift))
        weight = weight + probs[j].sum(axis=0, keepdims=True)
        low.append(probs[j].astype(BF16))
        total = total + dot_nn(vt[j], low[j])
    inverse = 1.0 / weight
    head_out = (total * inverse).astype(BF16)
    out_ref[0] = head_out
    grads_f = dot_ref[0].astype(F32)
    row_dot = jnp.sum(grads_f * head_out.astype(F32), axis=0, keepdims=True)
    lse_ref[0] = jnp.broadcast_to(top + jnp.log2(weight), lse_ref.shape[1:])
    row_dot_ref[0] = jnp.broadcast_to(row_dot, row_dot_ref.shape[1:])
    grads_low = (grads_f * inverse).astype(BF16)
    grads_rows = grads_low.T
    shift_dot = row_dot * inverse
    dq = None
    for j in range(2):
        grad_probs = dot_nn(values[j], grads_low)
        grad_scores = (probs[j] * (grad_probs - shift_dot)).astype(BF16)
        dv_acc[j] += dot_nn(low[j], grads_rows)
        dk_acc[j] += dot_nn(grad_scores, q_ref[0])
        term = dot_nn(kt[j], grad_scores)
        dq = term if dq is None else dq + term
    dq_ref[0] = dq

    @pl.when(step == tiles - 1)
    def _():
        for j in range(2):
            dnear_ref[0, 0, :, j] = (
                (dk_acc[j] * softmax_scale).astype(BF16).reshape(groups, piece, width)
            )
            dnear_ref[0, 1, :, j] = dv_acc[j].astype(BF16).reshape(groups, piece, width)


def near_attention(seen, queries, turned_q, turned_do, near, own_out, own_lse, softmax_scale, tile):
    kv_count, rows, width = queries.shape
    tiles = rows // tile
    _, _, groups, _, piece, _ = near.shape
    key_rows = groups * piece
    by_row = pl.BlockSpec((1, tile, width), lambda n, i: (n, i, 0))
    turned = pl.BlockSpec((1, width, tile), lambda n, i: (n, 0, i))
    stat = pl.BlockSpec((1, 8, tile), lambda n, i: (n, 0, i))
    by_head = pl.BlockSpec((1,) + near.shape[1:], lambda n, i: (n, 0, 0, 0, 0, 0))
    return pl.pallas_call(
        functools.partial(near_kernel, softmax_scale, tiles),
        grid=(kv_count, tiles),
        out_shape=(
            jax.ShapeDtypeStruct((kv_count, width, rows), BF16),
            jax.ShapeDtypeStruct((kv_count, 8, rows), F32),
            jax.ShapeDtypeStruct((kv_count, 8, rows), F32),
            jax.ShapeDtypeStruct((kv_count, width, rows), F32),
            jax.ShapeDtypeStruct(near.shape, BF16),
        ),
        in_specs=[
            pl.BlockSpec(memory_space=pltpu.SMEM),
            by_row,
            turned,
            turned,
            by_head,
            turned,
            stat,
        ],
        out_specs=(turned, stat, stat, turned, by_head),
        scratch_shapes=[
            pltpu.VMEM((2, key_rows, width), F32),
            pltpu.VMEM((2, key_rows, width), F32),
            pltpu.VMEM((2, width, key_rows), BF16),
            pltpu.VMEM((2, width, key_rows), BF16),
        ],
        compiler_params=pltpu.CompilerParams(vmem_limit_bytes=GRANT),
        cost_estimate=pl.CostEstimate(
            flops=20 * kv_count * rows * key_rows * width,
            bytes_accessed=20 * kv_count * rows * width,
            transcendentals=2 * kv_count * rows * key_rows,
        ),
        name="near_attention",
    )(seen, queries, turned_q, turned_do, near, own_out, own_lse)


def own_backward_kernel(
    softmax_scale,
    groups,
    q_ref,
    do_ref,
    qt_ref,
    dot_ref,
    kv_ref,
    lse_ref,
    row_dot_ref,
    out_t_ref,
    dq_near_ref,
    rows_ref,
    dkv_ref,
    kt,
):
    log_scale = softmax_scale * math.log2(math.e)
    half = kv_ref.shape[2] // 2
    step = pl.program_id(1)
    seen = causal_pairs(half)

    @pl.when(step == 0)
    def _():
        dkv_ref[...] = jnp.zeros_like(dkv_ref)
        kt[...] = kv_ref[0, 0].T

    rows_ref[0, 0, 0] = out_t_ref[0].T
    for tile in range(2):
        span = slice(tile * half, (tile + 1) * half)
        query = qt_ref[0, :, span]
        grads = dot_ref[0, :, span]
        lse = lse_ref[0, :1, span]
        row_dot = row_dot_ref[0, :1, span]
        dq = dq_near_ref[0, :, span]
        for col in range(tile + 1):
            cols = slice(col * half, (col + 1) * half)
            probs = jnp.exp2(dot_nn(kv_ref[0, 0, cols, :], query) * log_scale - lse)
            if col == tile:
                probs = jnp.where(seen, probs, 0.0)
            grad_probs = dot_nn(kv_ref[0, 1, cols, :], grads)
            grad_scores = (probs * (grad_probs - row_dot)).astype(BF16)
            dq = dq + dot_nn(kt[:, cols], grad_scores)
            dkv_ref[0, 0, cols, :] += dot_nn(grad_scores, q_ref[0, 0, span, :])
            dkv_ref[0, 1, cols, :] += dot_nn(probs.astype(BF16), do_ref[0, 0, span, :])
        rows_ref[1, 0, 0, span, :] = (dq * softmax_scale).astype(BF16).T

    @pl.when(step == groups - 1)
    def _():
        dkv_ref[0, 0] = dkv_ref[0, 0] * softmax_scale


def own_backward(
    queries, grads, turned_q, turned_do, own_kv, lse, row_dot, turned_out, dq_near, softmax_scale
):
    kv_count, groups, rows, width = queries.shape
    by_group = pl.BlockSpec((1, 1, rows, width), lambda n, g: (n, g, 0, 0))
    by_head = pl.BlockSpec((1, 2, rows, width), lambda n, g: (n, 0, 0, 0))
    turned = pl.BlockSpec((1, width, rows), lambda n, g: (n, 0, g))
    stat = pl.BlockSpec((1, 8, rows), lambda n, g: (n, 0, g))
    return pl.pallas_call(
        functools.partial(own_backward_kernel, softmax_scale, groups),
        grid=(kv_count, groups),
        out_shape=(
            jax.ShapeDtypeStruct((2,) + queries.shape, BF16),
            jax.ShapeDtypeStruct(own_kv.shape, F32),
        ),
        in_specs=[by_group, by_group, turned, turned, by_head, stat, stat, turned, turned],
        out_specs=(pl.BlockSpec((2, 1, 1, rows, width), lambda n, g: (0, n, g, 0, 0)), by_head),
        scratch_shapes=[pltpu.VMEM((width, rows), BF16)],
        compiler_params=pltpu.CompilerParams(vmem_limit_bytes=GRANT),
        cost_estimate=pl.CostEstimate(
            flops=10 * kv_count * groups * rows * rows * width,
            bytes_accessed=16 * kv_count * groups * rows * width,
            transcendentals=kv_count * groups * rows * rows,
        ),
        name="own_backward",
    )(queries, grads, turned_q, turned_do, own_kv, lse, row_dot, turned_out, dq_near)


def exchange(pieces):
    return lax.ppermute(pieces, "head", [(0, 1), (1, 0)])


def spread(pieces):
    return lax.all_to_all(pieces, "ctx", split_axis=0, concat_axis=0, tiled=True)


def on_device(queries, keys, values, output_gradient, selected):
    rows_block, own_groups, kv_count, width = queries.shape
    blocks = lax.axis_size("ctx")
    own_index = lax.axis_index("ctx")
    core = lax.axis_index("head")
    half_kv = kv_count // 2
    mine, theirs = core * half_kv, (1 - core) * half_kv
    softmax_scale = width ** (-0.5)
    piece_groups = blocks // (2 * half_kv)
    piece = rows_block // piece_groups
    picks = selected.reshape(-1)
    own_picks = lax.dynamic_index_in_dim(selected, own_index, 0, keepdims=False)
    seen = (own_picks < own_index).astype(jnp.int32)

    both = jnp.stack([keys, values], axis=0)
    both = lax.dynamic_slice_in_dim(both, mine, half_kv, axis=2)
    own_kv = jnp.transpose(both, (2, 0, 1, 3))
    held = spread(own_kv.reshape(blocks, piece, width))

    inputs = jnp.transpose(jnp.stack([queries, output_gradient], axis=0), (0, 3, 2, 1, 4))
    kept = lax.dynamic_slice_in_dim(inputs, mine, half_kv, axis=1)
    fetched = exchange(lax.dynamic_slice_in_dim(inputs, theirs, half_kv, axis=1))
    inputs = jnp.concatenate([kept, fetched], axis=2)
    q_all, do_all = inputs[0], inputs[1]
    turned_q, turned_do, own_out, own_lse = own_forward(q_all, do_all, own_kv, softmax_scale)

    near = spread(pick_pieces(held, picks))
    near = near.reshape(half_kv, 2, piece_groups, 2, piece, width)
    group_rows = 2 * own_groups * rows_block
    turned_out, lse, row_dot, dq_near, dnear = near_attention(
        seen,
        q_all.reshape(half_kv, group_rows, width),
        turned_q,
        turned_do,
        near,
        own_out,
        own_lse,
        softmax_scale,
        group_rows // 2,
    )
    arrived = spread(dnear.reshape(blocks, 2 * piece, width))
    results, dkv = own_backward(
        q_all,
        do_all,
        turned_q,
        turned_do,
        own_kv,
        lse,
        row_dot,
        turned_out,
        dq_near,
        softmax_scale,
    )
    home = spread(collect_pieces(arrived, picks))

    back = exchange(results[:, :, own_groups:])
    whole = jnp.zeros((2, kv_count) + back.shape[2:], results.dtype)
    whole = lax.dynamic_update_slice_in_dim(whole, results[:, :, :own_groups], mine, 1)
    whole = lax.dynamic_update_slice_in_dim(whole, back, theirs, 1)
    attn_out, grad_q = (jnp.transpose(whole[part], (2, 1, 0, 3)) for part in range(2))
    grads = (home.reshape(own_kv.shape).astype(F32) + dkv).astype(BF16)
    grad_k, grad_v = (jnp.transpose(grads[:, part], (1, 0, 2)) for part in range(2))
    return (attn_out, grad_q, grad_k, grad_v)


def solution(mesh):
    return jax.shard_map(
        on_device,
        mesh=mesh,
        in_specs=(
            P("ctx", "head", None, None),
            P("ctx", None, None),
            P("ctx", None, None),
            P("ctx", "head", None, None),
            P(),
        ),
        out_specs=(
            P("ctx", "head", None, None),
            P("ctx", "head", None, None),
            P("ctx", "head", None),
            P("ctx", "head", None),
        ),
        check_vma=False,
    )
```

time: 175 us -> 159 us (0.909)
  local copies, waits for them, and re-layouts: 28.7 us -> 12.9 us
  Pallas kernels: 47.1 us -> 44.5 us
    unnamed x42 -> x11, local copies, waits for them, and re-layouts: 17.2 us -> 2.08 us
    pallas_call x1, Pallas kernels: 25.6 us -> 18.6 us  [near_attention(): pl.pallas_call(functools.partial(near_kernel, softmax_scale, tiles), grid...]
    pallas_call x1, Pallas kernels: 6.22 us -> 9.41 us  [own_forward(): pl.pallas_call(functools.partial(own_forward_kernel, softmax_scale * math...]
    squeeze x0 -> x1, other arithmetic: none -> 2.7 us  [on_device(): q_all, do_all = (inputs[0], inputs[1])]
    pallas_call x1, Pallas kernels: 9.81 us -> 12 us  [own_backward(): pl.pallas_call(functools.partial(own_backward_kernel, softmax_scale, grou...]
    all_to_all x4, waiting for transfers between devices: 54.8 us -> 57 us  [spread(): lax.all_to_all(pieces, 'ctx', split_axis=0, concat_axis=0, tiled=True)]
    transpose x0 -> x1, local copies, waits for them, and re-layouts: none -> 2.04 us  [on_device(): jnp.transpose(whole[part], (2, 1, 0, 3))]
    dynamic_update_slice x4 -> x2, local copies, waits for them, and re-layouts: 5.34 us -> 3.61 us  [the longest x1 1.8 us: on_device(): whole = lax.dynamic_update_slice_in_dim(whole, back, theirs, 1)]
  transfers between devices with their start and end apart: 7 -> 6, of which waited for: 5 -> 5; matrix products, arithmetic and copies ran while one was open for 8% -> 9% of each run, Pallas kernels for 11% -> 15%
where the time goes in v1:
time: 159 us; the launch traced here: 158 us
  waiting for transfers between devices  58.2 us (37%)
  Pallas kernels  44.5 us (28%)
  starting transfers between devices  36.4 us (23%)
  local copies, waits for them, and re-layouts  12.9 us (8%)
  other arithmetic  5.44 us (3%)
    all_to_all x4, waiting for transfers between devices, spread(): lax.all_to_all(pieces, 'ctx', split_axis=0, concat_axis=0, tiled=True)  57 us
    all_to_all x4, starting transfers between devices, spread(): lax.all_to_all(pieces, 'ctx', split_axis=0, concat_axis=0, tiled=True)  36.3 us
    pallas_call x1, Pallas kernels, near_attention(): pl.pallas_call(functools.partial(near_kernel, softmax_scale, tiles), grid...  18.6 us
    pallas_call x1, Pallas kernels, own_backward(): pl.pallas_call(functools.partial(own_backward_kernel, softmax_scale, grou...  12 us
    pallas_call x1, Pallas kernels, own_forward(): pl.pallas_call(functools.partial(own_forward_kernel, softmax_scale * math...  9.41 us
  transfers between devices with their start and end apart: 6, of which 5 were waited for; matrix products, arithmetic and copies ran while one was open for 9% of the time, Pallas kernels for 15%

profile of v1, /device:TPU:32, one launch (start us, length us, event | category | flops | bytes accessed | tf_op | source)
XLA Modules:
  0.0 158.1 jit_solution(2562671988117443241)
XLA Ops:
  0.6 1.3 copy_bitcast_fusion.2
  2.0 0.9 fusion.7
  2.8 15.0 %all-to-all-start = ((bf16[128,16,128]{2,1,0:T(8,128)(2,1)}), bf16[128,16,128]{2,1,0:T(8,128)(2,1)S(1)}, u32[]{:S(2)}, u32[]{:S(2)}) async-start(bf16[128,16,128]{2,1,0:T(8,128)(2,1)} %bitcast.10), calls=%async_computation | async-start | bytes 1048576 | tf_op jit(solution)/shard_map/all_to_all | solution.py:384
  18.1 19.8 %all-to-all-done.held = bf16[128,16,128]{2,1,0:T(8,128)(2,1)S(1)} async-done(((bf16[128,16,128]{2,1,0:T(8,128)(2,1)}), bf16[128,16,128]{2,1,0:T(8,128)(2,1)S(1)}, u32[]{:S(2)}, u32[]{:S(2)}) %all-to-all-start) | async-done | bytes 524320 | tf_op jit(solution)/shard_map/all_to_all | solution.py:384
  38.0 1.8 %pick_pieces.1 = bf16[128,32,128]{2,1,0:T(8,128)(2,1)} custom-call(s32[256]{0:T(256)S(1)} %reshape.27.picks, bf16[128,16,128]{2,1,0:T(8,128)(2,1)S(1)} %all-to-all-done.held), custom_call_target="tpu_custom_call" | custom-call | tf_op jit(solution)/shard_map/pick_pieces/pallas_call | solution.py:47
  39.8 7.8 %all-to-all-start.1 = ((bf16[128,32,128]{2,1,0:T(8,128)(2,1)}), bf16[128,32,128]{2,1,0:T(8,128)(2,1)}, u32[]{:S(2)}, u32[]{:S(2)}) async-start(bf16[128,32,128]{2,1,0:T(8,128)(2,1)} %pick_pieces.1), calls=%async_computation.1 | async-start | bytes 2097152 | tf_op jit(solution)/shard_map/all_to_all | solution.py:384
  49.1 0.8 fusion.10.kv_ref
  49.9 1.2 collective-permute-done
  51.1 2.7 %fusion.5 = (bf16[2,4,512,128]{3,2,1,0:T(8,128)(2,1)}, bf16[1,2,4,512,128]{4,3,2,1,0:T(8,128)(2,1)}) fusion(bf16[2,2,2,512,128]{4,3,2,1,0:T(8,128)(2,1)} %collective-permute-done, bf16[2,2,2,512,128]{4,3,2,1,0:T(8,128)(2,1)S(1)} %get-tuple-element.41), kind=kLoop, calls=%fused_computation.14 | loop fusion | flops 1048576 | bytes 4194304 | tf_op jit(solution)/shard_map/squeeze | solution.py:410
  53.8 9.4 %own_forward.1 = (bf16[2,128,2048]{2,1,0:T(8,128)(2,1)}, bf16[2,128,2048]{2,1,0:T(8,128)(2,1)}, f32[2,128,2048]{2,1,0:T(8,128)}, f32[2,8,2048]{2,1,0:T(8,128)}) custom-call(bf16[2,4,512,128]{3,2,1,0:T(8,128)(2,1)} %bitcast.42, bf16[2,4,512,128]{3,2,1,0:T(8,128)(2,1)} %get-tuple-element.38.do_ref, bf16[2,2,512,128]{3,2,1,0:T(8,128)(2,1)} %fusion.10.kv_ref), custom_call_target="tpu_custom_call" | custom-call | flops 1073741824 | bytes 6291456 | tf_op jit(solution)/shard_map/own_forward/pallas_call | solution.py:147
  63.2 13.9 %all-to-all-done.1 = bf16[128,32,128]{2,1,0:T(8,128)(2,1)} async-done(((bf16[128,32,128]{2,1,0:T(8,128)(2,1)}), bf16[128,32,128]{2,1,0:T(8,128)(2,1)}, u32[]{:S(2)}, u32[]{:S(2)}) %all-to-all-start.1) | async-done | bytes 1048608 | tf_op jit(solution)/shard_map/all_to_all | solution.py:384
  77.1 18.6 %near_attention.1 = (bf16[2,128,2048]{2,1,0:T(8,128)(2,1)}, f32[2,8,2048]{2,1,0:T(8,128)}, f32[2,8,2048]{2,1,0:T(8,128)}, f32[2,128,2048]{2,1,0:T(8,128)}, bf16[2,2,32,2,16,128]{5,4,3,2,1,0:T(8,128)(2,1)}) custom-call(s32[2]{0:T(128)} %fusion.8.seen_ref, bf16[2,2048,128]{2,1,0:T(8,128)(2,1)} %bitcast.43, bf16[2,128,2048]{2,1,0:T(8,128)(2,1)} %get-tuple-element.15.qt_ref, ...), custom_call_target="tpu_custom_call" | custom-call | flops 5368709120 | bytes 10485760 | tf_op jit(solution)/shard_map/near_attention/pallas_call | solution.py:264
  95.8 6.8 %all-to-all-start.2 = ((bf16[128,32,128]{2,1,0:T(8,128)(2,1)}), bf16[128,32,128]{2,1,0:T(8,128)(2,1)S(1)}, u32[]{:S(2)}, u32[]{:S(2)}) async-start(bf16[128,32,128]{2,1,0:T(8,128)(2,1)} %bitcast.41), calls=%async_computation.2 | async-start | bytes 2097152 | tf_op jit(solution)/shard_map/all_to_all | solution.py:384
  102.6 12.0 %own_backward.1 = (bf16[2,2,4,512,128]{4,3,2,1,0:T(8,128)(2,1)}, f32[2,2,512,128]{3,2,1,0:T(8,128)}) custom-call(bf16[2,4,512,128]{3,2,1,0:T(8,128)(2,1)} %bitcast.44, bf16[2,4,512,128]{3,2,1,0:T(8,128)(2,1)} %get-tuple-element.38.do_ref, bf16[2,128,2048]{2,1,0:T(8,128)(2,1)} %get-tuple-element.15.qt_ref, bf16[2,128,2048]{2,1,0:T(8,128)(2,1)} %get-tuple-element.16.dot_ref, ...), custom_call_target="tpu_custom_call" | custom-call | flops 2684354560 | bytes 8388608 | tf_op jit(solution)/shard_map/own_backward/pallas_call | solution.py:359
  114.6 2.7 %fusion.9 = (bf16[2,2,2,512,128]{4,3,2,1,0:T(8,128)(2,1)}, bf16[2,2,2,512,128]{4,3,2,1,0:T(8,128)(2,1)S(1)}) fusion(bf16[2,2,4,512,128]{4,3,2,1,0:T(8,128)(2,1)} %get-tuple-element.23), kind=kLoop, calls=%fused_computation.31 | loop fusion | bytes 4194304 | tf_op jit(solution)/shard_map/slice | solution.py:442
  117.3 13.4 %all-to-all-done.2.arrived = bf16[128,32,128]{2,1,0:T(8,128)(2,1)S(1)} async-done(((bf16[128,32,128]{2,1,0:T(8,128)(2,1)}), bf16[128,32,128]{2,1,0:T(8,128)(2,1)S(1)}, u32[]{:S(2)}, u32[]{:S(2)}) %all-to-all-start.2) | async-done | bytes 1048608 | tf_op jit(solution)/shard_map/all_to_all | solution.py:384
  130.7 2.7 %collect_pieces.1 = bf16[128,16,128]{2,1,0:T(8,128)(2,1)} custom-call(s32[256]{0:T(256)S(1)} %reshape.27.picks, bf16[128,32,128]{2,1,0:T(8,128)(2,1)S(1)} %all-to-all-done.2.arrived), custom_call_target="tpu_custom_call" | custom-call | tf_op jit(solution)/shard_map/collect_pieces/pallas_call | solution.py:88
  133.4 6.6 %all-to-all-start.3 = ((bf16[128,16,128]{2,1,0:T(8,128)(2,1)}), bf16[128,16,128]{2,1,0:T(8,128)(2,1)S(1)}, u32[]{:S(2)}, u32[]{:S(2)}) async-start(bf16[128,16,128]{2,1,0:T(8,128)(2,1)} %collect_pieces.1), calls=%async_computation.3 | async-start | bytes 1048576 | tf_op jit(solution)/shard_map/all_to_all | solution.py:384
  140.6 1.8 %copy_dynamic-update-slice_fusion.1 = bf16[2,4,2,512,128]{4,1,2,3,0:T(4,128)(2,1)S(1)} fusion(bf16[2,4,2,512,128]{4,1,2,3,0:T(4,128)(2,1)S(1)} %broadcast_in_dim.3, s32[]{:T(128)S(6)} %select_n.13, bf16[2,2,2,512,128]{4,3,2,1,0:T(8,128)(2,1)S(1)} %get-tuple-element.37), kind=kLoop, calls=%fused_computation.20 | loop fusion | bytes 2097156 | tf_op jit(solution)/shard_map/dynamic_update_slice | solution.py:444
  142.4 1.8 %copy_dynamic-update-slice_fusion = bf16[2,4,2,512,128]{4,1,2,3,0:T(4,128)(2,1)S(1)} fusion(bf16[2,4,2,512,128]{4,1,2,3,0:T(4,128)(2,1)S(1)} %copy_dynamic-update-slice_fusion.1, s32[]{:T(128)S(6)} %select_n.14, bf16[2,2,2,512,128]{4,3,2,1,0:T(8,128)(2,1)S(1)} %collective-permute-done.1), kind=kLoop, calls=%fused_computation.19 | loop fusion | bytes 2097156 | tf_op jit(solution)/shard_map/dynamic_update_slice | solution.py:445
  144.2 2.0 %slice_bitcast_fusion = (bf16[512,2,4,128]{3,2,1,0:T(4,128)(2,1)}, bf16[512,2,4,128]{3,2,1,0:T(4,128)(2,1)}) fusion(bf16[2,4,2,512,128]{4,1,2,3,0:T(4,128)(2,1)S(1)} %copy_dynamic-update-slice_fusion), kind=kLoop, calls=%fused_computation.11 | loop fusion | bytes 4194304 | tf_op jit(solution)/shard_map/transpose | solution.py:446
  146.2 9.8 %all-to-all-done.3 = bf16[128,16,128]{2,1,0:T(8,128)(2,1)S(1)} async-done(((bf16[128,16,128]{2,1,0:T(8,128)(2,1)}), bf16[128,16,128]{2,1,0:T(8,128)(2,1)S(1)}, u32[]{:S(2)}, u32[]{:S(2)}) %all-to-all-start.3) | async-done | bytes 524320 | tf_op jit(solution)/shard_map/all_to_all | solution.py:384
  156.2 1.0 copy.24
  157.2 1.0 copy.25
  (19 shorter events, 2.4 us)
Async XLA Ops:
  0.6 17.2 %copy-start.3 = (s32[128,2]{0,1:T(2,128)S(1)}, s32[128,2]{0,1:T(2,128)}, u32[]{:S(2)}) copy-start(s32[128,2]{0,1:T(2,128)} %param.9) | copy-start | bytes 3076
  2.8 35.1 %all-to-all-start = ((bf16[128,16,128]{2,1,0:T(8,128)(2,1)}), bf16[128,16,128]{2,1,0:T(8,128)(2,1)S(1)}, u32[]{:S(2)}, u32[]{:S(2)}) async-start(bf16[128,16,128]{2,1,0:T(8,128)(2,1)} %bitcast.10), calls=%async_computation | async-start | bytes 1048576 | tf_op jit(solution)/shard_map/all_to_all | solution.py:384
  17.9 29.7 %copy-start.1 = (bf16[512,2,4,128]{3,2,1,0:T(4,128)(2,1)S(1)}, bf16[512,2,4,128]{3,2,1,0:T(4,128)(2,1)}, u32[]{:S(2)}) copy-start(bf16[512,2,4,128]{3,2,1,0:T(4,128)(2,1)} %param.8) | copy-start | bytes 3145732
  39.8 7.8 %copy-start.2 = (bf16[512,2,4,128]{3,2,1,0:T(4,128)(2,1)S(1)}, bf16[512,2,4,128]{3,2,1,0:T(4,128)(2,1)}, u32[]{:S(2)}) copy-start(bf16[512,2,4,128]{3,2,1,0:T(4,128)(2,1)} %param.5) | copy-start | bytes 3145732
  39.8 37.4 %all-to-all-start.1 = ((bf16[128,32,128]{2,1,0:T(8,128)(2,1)}), bf16[128,32,128]{2,1,0:T(8,128)(2,1)}, u32[]{:S(2)}, u32[]{:S(2)}) async-start(bf16[128,32,128]{2,1,0:T(8,128)(2,1)} %pick_pieces.1), calls=%async_computation.1 | async-start | bytes 2097152 | tf_op jit(solution)/shard_map/all_to_all | solution.py:384
  48.2 2.9 %collective-permute-start = (bf16[2,2,2,512,128]{4,3,2,1,0:T(8,128)(2,1)S(1)}, bf16[2,2,2,512,128]{4,3,2,1,0:T(8,128)(2,1)}, u32[]{:S(2)}, u32[]{:S(2)}) collective-permute-start(bf16[2,2,2,512,128]{4,3,2,1,0:T(8,128)(2,1)S(1)} %get-tuple-element.40), channel_id=1, source_target_pairs={{0,1},{1,0},{2,3},{3,2},{4,5},{5,4},{6,7},{7,6},{8,9},{9,8},{10,11... | collective-permute-start | bytes 3145736 | tf_op jit(solution)/shard_map/ppermute | solution.py:380
  95.8 35.0 %all-to-all-start.2 = ((bf16[128,32,128]{2,1,0:T(8,128)(2,1)}), bf16[128,32,128]{2,1,0:T(8,128)(2,1)S(1)}, u32[]{:S(2)}, u32[]{:S(2)}) async-start(bf16[128,32,128]{2,1,0:T(8,128)(2,1)} %bitcast.41), calls=%async_computation.2 | async-start | bytes 2097152 | tf_op jit(solution)/shard_map/all_to_all | solution.py:384
  117.3 25.0 %collective-permute-start.1 = (bf16[2,2,2,512,128]{4,3,2,1,0:T(8,128)(2,1)}, bf16[2,2,2,512,128]{4,3,2,1,0:T(8,128)(2,1)S(1)}, u32[]{:S(2)}, u32[]{:S(2)}) collective-permute-start(bf16[2,2,2,512,128]{4,3,2,1,0:T(8,128)(2,1)} %get-tuple-element.36), channel_id=1, source_target_pairs={{0,1},{1,0},{2,3},{3,2},{4,5},{5,4},{6,7},{7,6},{8,9},{9,8},{10,11... | collective-permute-start | bytes 3145736 | tf_op jit(solution)/shard_map/ppermute | solution.py:380
  133.4 22.7 %all-to-all-start.3 = ((bf16[128,16,128]{2,1,0:T(8,128)(2,1)}), bf16[128,16,128]{2,1,0:T(8,128)(2,1)S(1)}, u32[]{:S(2)}, u32[]{:S(2)}) async-start(bf16[128,16,128]{2,1,0:T(8,128)(2,1)} %collect_pieces.1), calls=%async_computation.3 | async-start | bytes 1048576 | tf_op jit(solution)/shard_map/all_to_all | solution.py:384
  144.2 11.9 %copy-start = (f32[2,2,512,128]{3,2,1,0:T(8,128)S(1)}, f32[2,2,512,128]{3,2,1,0:T(8,128)}, u32[]{:S(2)}) copy-start(f32[2,2,512,128]{3,2,1,0:T(8,128)} %get-tuple-element.25) | copy-start | bytes 3145732

commit v2 on v1

v2 whole, which is shorter than its diff:
```python
import functools
import math

import jax
import jax.numpy as jnp
from jax import lax
from jax.experimental import pallas as pl
from jax.experimental.pallas import tpu as pltpu
from jax.sharding import PartitionSpec as P

F32 = jnp.float32
BF16 = jnp.bfloat16
GRANT = 60 * 1024 * 1024
SMALL_GRANT = 8 * 1024 * 1024


def dot_nn(a, b):
    return lax.dot_general(a, b, (((1,), (0,)), ((), ())), preferred_element_type=F32)


def dot_nt(a, b):
    return lax.dot_general(a, b, (((1,), (1,)), ((), ())), preferred_element_type=F32)


def dot_tn(a, b):
    return lax.dot_general(a, b, (((0,), (0,)), ((), ())), preferred_element_type=F32)


def pick_kernel(picks, held, out):
    count, rows2, _ = out.shape
    rows = rows2 // 2
    first = pl.program_id(0) * count

    def body(step, _):
        for sub in range(8):
            at = step * 8 + sub
            for j in range(2):
                out[at, j * rows : (j + 1) * rows, :] = held[picks[(first + at) * 2 + j]]
        return 0

    lax.fori_loop(0, count // 8, body, 0)


def pick_pieces(held, picks):
    blocks, rows, width = held.shape
    steps = 2 if blocks % 16 == 0 else 1
    return pl.pallas_call(
        pick_kernel,
        grid=(steps,),
        out_shape=jax.ShapeDtypeStruct((blocks, 2 * rows, width), held.dtype),
        in_specs=[
            pl.BlockSpec(memory_space=pltpu.SMEM),
            pl.BlockSpec((blocks, rows, width), lambda i: (0, 0, 0)),
        ],
        out_specs=pl.BlockSpec((blocks // steps, 2 * rows, width), lambda i: (i, 0, 0)),
        compiler_params=pltpu.CompilerParams(vmem_limit_bytes=SMALL_GRANT),
        name="pick_pieces",
    )(picks, held)


def collect_kernel(picks, arrived, out, *totals):
    count, rows2, _ = arrived.shape
    rows = rows2 // 2
    part = pl.program_id(0)

    @pl.when(part == 0)
    def _():
        for total in totals:
            total[...] = jnp.zeros_like(total)

    def body(step, _):
        for sub in range(8):
            at = step * 8 + sub
            for j in range(2):
                owner = picks[(part * count + at) * 2 + j]
                totals[j][owner] += arrived[at, j * rows : (j + 1) * rows, :].astype(F32)
        return 0

    lax.fori_loop(0, count // 8, body, 0)

    @pl.when(part == pl.num_programs(0) - 1)
    def _():
        out[...] = (totals[0][...] + totals[1][...]).astype(out.dtype)


def collect_pieces(arrived, picks):
    blocks, rows2, width = arrived.shape
    steps = 2 if blocks % 16 == 0 else 1
    return pl.pallas_call(
        collect_kernel,
        grid=(steps,),
        out_shape=jax.ShapeDtypeStruct((blocks, rows2 // 2, width), arrived.dtype),
        in_specs=[
            pl.BlockSpec(memory_space=pltpu.SMEM),
            pl.BlockSpec((blocks // steps, rows2, width), lambda i: (i, 0, 0)),
        ],
        out_specs=pl.BlockSpec((blocks, rows2 // 2, width), lambda i: (0, 0, 0)),
        scratch_shapes=[pltpu.VMEM((blocks, rows2 // 2, width), F32)] * 2,
        compiler_params=pltpu.CompilerParams(vmem_limit_bytes=SMALL_GRANT),
        name="collect_pieces",
    )(picks, arrived)


def causal_pairs(rows):
    return lax.broadcasted_iota(jnp.int32, (rows, rows), 0) <= lax.broadcasted_iota(
        jnp.int32, (rows, rows), 1
    )


def own_forward_kernel(log_scale, q_ref, do_ref, kv_ref, qt_ref, dot_ref, lse_ref, row_dot_ref, vt):
    width = kv_ref.shape[3]
    half = kv_ref.shape[2] // 2
    seen = causal_pairs(half)

    @pl.when(pl.program_id(1) == 0)
    def _():
        vt[...] = kv_ref[0, 1].T

    turned_do = do_ref[0, 0].T
    qt_ref[0] = q_ref[0, 0].T
    dot_ref[0] = turned_do
    for tile in range(2):
        span = slice(tile * half, (tile + 1) * half)
        query = qt_ref[0, :, span]
        parts = []
        for col in range(tile + 1):
            scores = dot_nn(kv_ref[0, 0, col * half : (col + 1) * half, :], query)
            if col == tile:
                scores = jnp.where(seen, scores, -jnp.inf)
            parts.append(scores)
        top = parts[0].max(axis=0, keepdims=True)
        for scores in parts[1:]:
            top = jnp.maximum(top, scores.max(axis=0, keepdims=True))
        top = top * log_scale
        weight = jnp.zeros_like(top)
        total = jnp.zeros((width, half), F32)
        for col, scores in enumerate(parts):
            probs = jnp.exp2(scores * log_scale - top)
            weight = weight + probs.sum(axis=0, keepdims=True)
            total = total + dot_nn(vt[:, col * half : (col + 1) * half], probs.astype(BF16))
        row_dot = jnp.sum(total * turned_do[:, span].astype(F32), axis=0, keepdims=True) / weight
        lse_ref[0, :, span] = jnp.broadcast_to(top + jnp.log2(weight), (8, half))
        row_dot_ref[0, :, span] = jnp.broadcast_to(row_dot, (8, half))


def own_forward(queries, grads, own_kv, softmax_scale):
    kv_count, groups, rows, width = queries.shape
    by_group = pl.BlockSpec((1, 1, rows, width), lambda n, g: (n, g, 0, 0))
    turned = pl.BlockSpec((1, width, rows), lambda n, g: (n, 0, g))
    stat = pl.BlockSpec((1, 8, rows), lambda n, g: (n, 0, g))
    return pl.pallas_call(
        functools.partial(own_forward_kernel, softmax_scale * math.log2(math.e)),
        grid=(kv_count, groups),
        out_shape=(
            jax.ShapeDtypeStruct((kv_count, width, groups * rows), BF16),
            jax.ShapeDtypeStruct((kv_count, width, groups * rows), BF16),
            jax.ShapeDtypeStruct((kv_count, 8, groups * rows), F32),
            jax.ShapeDtypeStruct((kv_count, 8, groups * rows), F32),
        ),
        in_specs=[
            by_group,
            by_group,
            pl.BlockSpec((1, 2, rows, width), lambda n, g: (n, 0, 0, 0)),
        ],
        out_specs=(turned, turned, stat, stat),
        scratch_shapes=[pltpu.VMEM((width, rows), BF16)],
        compiler_params=pltpu.CompilerParams(vmem_limit_bytes=GRANT),
        cost_estimate=pl.CostEstimate(
            flops=4 * kv_count * groups * rows * rows * width,
            bytes_accessed=12 * kv_count * groups * rows * width,
            transcendentals=kv_count * groups * rows * rows,
        ),
        name="own_forward",
    )(queries, grads, own_kv)


def near_kernel(
    softmax_scale,
    tile,
    seen_ref,
    qt_ref,
    dot_ref,
    near_ref,
    own_lse_ref,
    own_dot_ref,
    lse_ref,
    row_dot_ref,
    dnear_ref,
    dk_acc,
    dv_acc,
):
    log_scale = softmax_scale * math.log2(math.e)
    groups, _, piece, width = near_ref.shape[2:]
    rows = groups * piece
    seen = [seen_ref[j] > 0 for j in range(2)]
    count = qt_ref.shape[2] // tile
    held = [{} for _ in range(count)]
    dk_acc[...] = jnp.zeros_like(dk_acc)
    dv_acc[...] = jnp.zeros_like(dv_acc)

    def span(at):
        return slice(at * tile, (at + 1) * tile)

    def score(at, j):
        scores = dot_nn(near_ref[0, 0, :, j].reshape(rows, width), qt_ref[0, :, span(at)])
        held[at]["scores", j] = scores
        held[at]["peak", j] = scores.max(axis=0, keepdims=True) * log_scale

    def settle(at):
        own_lse = own_lse_ref[0, :1, span(at)]
        top = own_lse
        for j in range(2):
            top = jnp.maximum(top, jnp.where(seen[j], held[at].pop(("peak", j)), -jnp.inf))
        share = jnp.exp2(own_lse - top)
        held[at]["top"] = top
        held[at]["weight"] = share
        held[at]["dot"] = share * own_dot_ref[0, :1, span(at)]

    def weigh(at, j):
        grad_probs = dot_nn(near_ref[0, 1, :, j].reshape(rows, width), dot_ref[0, :, span(at)])
        shift = jnp.where(seen[j], held[at]["top"], jnp.inf)
        probs = jnp.exp2(held[at].pop(("scores", j)) * log_scale - shift)
        held[at]["weight"] += probs.sum(axis=0, keepdims=True)
        held[at]["dot"] += (probs * grad_probs).sum(axis=0, keepdims=True)
        held[at]["low", j] = probs.astype(BF16)
        held[at]["grad_probs", j] = grad_probs

    def normalise(at):
        weight = held[at]["weight"]
        inverse = 1.0 / weight
        row_dot = held[at]["dot"] * inverse
        held[at]["row_dot"] = row_dot
        lse = held[at]["top"] + jnp.log2(weight)
        lse_ref[0, :, span(at)] = jnp.broadcast_to(lse, (8, tile))
        row_dot_ref[0, :, span(at)] = jnp.broadcast_to(row_dot, (8, tile))
        held[at]["grads"] = (dot_ref[0, :, span(at)].astype(F32) * inverse).astype(BF16).T
        held[at]["query"] = (qt_ref[0, :, span(at)].astype(F32) * inverse).astype(BF16).T

    def differ(at, j):
        change = held[at].pop(("grad_probs", j)) - held[at]["row_dot"]
        held[at]["grad_scores", j] = held[at]["low", j] * change.astype(BF16)

    def gather(at, j):
        dv_acc[j] += dot_nn(held[at].pop(("low", j)), held[at]["grads"])
        dk_acc[j] += dot_nn(held[at].pop(("grad_scores", j)), held[at]["query"])

    def stage(step, at, *parts):
        if 0 <= at < count:
            step(at, *parts)

    for at in range(count + 3):
        stage(settle, at - 1)
        stage(normalise, at - 2)
        for j in range(2):
            stage(gather, at - 3, j)
            stage(score, at, j)
            stage(weigh, at - 1, j)
            stage(differ, at - 2, j)

    for j in range(2):
        dnear_ref[0, 0, :, j] = (
            (dk_acc[j] * softmax_scale).astype(BF16).reshape(groups, piece, width)
        )
        dnear_ref[0, 1, :, j] = dv_acc[j].astype(BF16).reshape(groups, piece, width)


def near_attention(seen, turned_q, turned_do, near, own_lse, own_dot, softmax_scale, tile):
    kv_count, width, rows = turned_q.shape
    _, _, groups, _, piece, _ = near.shape
    key_rows = groups * piece
    turned = pl.BlockSpec((1, width, rows), lambda n: (n, 0, 0))
    stat = pl.BlockSpec((1, 8, rows), lambda n: (n, 0, 0))
    by_head = pl.BlockSpec((1,) + near.shape[1:], lambda n: (n, 0, 0, 0, 0, 0))
    return pl.pallas_call(
        functools.partial(near_kernel, softmax_scale, tile),
        grid=(kv_count,),
        out_shape=(
            jax.ShapeDtypeStruct((kv_count, 8, rows), F32),
            jax.ShapeDtypeStruct((kv_count, 8, rows), F32),
            jax.ShapeDtypeStruct(near.shape, BF16),
        ),
        in_specs=[pl.BlockSpec(memory_space=pltpu.SMEM), turned, turned, by_head, stat, stat],
        out_specs=(stat, stat, by_head),
        scratch_shapes=[
            pltpu.VMEM((2, key_rows, width), F32),
            pltpu.VMEM((2, key_rows, width), F32),
        ],
        compiler_params=pltpu.CompilerParams(vmem_limit_bytes=GRANT),
        cost_estimate=pl.CostEstimate(
            flops=16 * kv_count * rows * key_rows * width,
            bytes_accessed=10 * kv_count * rows * width,
            transcendentals=2 * kv_count * rows * key_rows,
        ),
        name="near_attention",
    )(seen, turned_q, turned_do, near, own_lse, own_dot)


def finish_kernel(
    softmax_scale,
    seen_ref,
    q_ref,
    do_ref,
    qt_ref,
    dot_ref,
    kv_ref,
    near_ref,
    lse_ref,
    row_dot_ref,
    kept_ref,
    moved_ref,
    dkv_ref,
    turned_kv,
):
    log_scale = softmax_scale * math.log2(math.e)
    group_count, block = q_ref.shape[1:3]
    groups, _, piece, width = near_ref.shape[2:]
    tile = block // 2
    triangle = causal_pairs(tile)
    dkv_ref[...] = jnp.zeros_like(dkv_ref)
    for kind in range(2):
        for j in range(2):
            turned_kv[kind, j] = near_ref[0, kind, :, j].reshape(block, width).T
        turned_kv[kind, 2] = kv_ref[0, kind].T
    items = []
    for at in range(group_count * 2):
        own = [(at, 2, col) for col in range(at % 2 + 1)]
        items += [(at, 0, None), (at, 1, None)] + own
    held = [{} for _ in items]
    sums = {}

    def keys_of(kind, j, col):
        if j < 2:
            return near_ref[0, kind, :, j].reshape(block, width)
        return kv_ref[0, kind, col * tile : (col + 1) * tile, :]

    def turned_of(kind, j, col):
        if j < 2:
            return turned_kv[kind, j]
        return turned_kv[kind, 2, :, col * tile : (col + 1) * tile]

    def score(item):
        at, j, col = items[item]
        held[item]["scores"] = dot_nn(keys_of(0, j, col), qt_ref[0, :, at * tile : (at + 1) * tile])

    def weigh(item):
        at, j, col = items[item]
        span = slice(at * tile, (at + 1) * tile)
        grad_probs = dot_nn(keys_of(1, j, col), dot_ref[0, :, span])
        lse = lse_ref[0, :1, span]
        if j < 2:
            lse = jnp.where(seen_ref[j] > 0, lse, jnp.inf)
        probs = jnp.exp2(held[item].pop("scores") * log_scale - lse)
        if j == 2 and col == at % 2:
            probs = jnp.where(triangle, probs, 0.0)
        held[item]["low"] = probs.astype(BF16)
        held[item]["grad_scores"] = (probs * (grad_probs - row_dot_ref[0, :1, span])).astype(BF16)

    def gather(item):
        at, j, col = items[item]
        low, grad_scores = held[item].pop("low"), held[item].pop("grad_scores")
        for kind, factor in ((1, low), (0, grad_scores)):
            term = dot_nn(turned_of(kind, j, col), factor)
            sums[at, kind] = sums[at, kind] + term if (at, kind) in sums else term
        group, rows = at // 2, slice(at % 2 * tile, (at % 2 + 1) * tile)
        if j == 2:
            cols = slice(col * tile, (col + 1) * tile)
            dkv_ref[0, 0, cols, :] += dot_nn(grad_scores, q_ref[0, group, rows, :])
            dkv_ref[0, 1, cols, :] += dot_nn(low, do_ref[0, group, rows, :])
            if col == at % 2:
                out_ref = kept_ref if 2 * group < group_count else moved_ref
                group = group % (group_count // 2)
                out_ref[0, 0, group, rows, :] = sums.pop((at, 1)).astype(BF16).T
                out_ref[1, 0, group, rows, :] = (
                    (sums.pop((at, 0)) * softmax_scale).astype(BF16).T
                )

    for item in range(len(items) + 2):
        for step, late in ((gather, 2), (score, 0), (weigh, 1)):
            if 0 <= item - late < len(items):
                step(item - late)
    dkv_ref[0, 0] = dkv_ref[0, 0] * softmax_scale


def finish(seen, queries, grads, turned_q, turned_do, own_kv, near, lse, row_dot, softmax_scale):
    kv_count, groups, rows, width = queries.shape
    by_head = pl.BlockSpec((1, groups, rows, width), lambda n: (n, 0, 0, 0))
    own = pl.BlockSpec((1, 2, rows, width), lambda n: (n, 0, 0, 0))
    turned = pl.BlockSpec((1, width, groups * rows), lambda n: (n, 0, 0))
    stat = pl.BlockSpec((1, 8, groups * rows), lambda n: (n, 0, 0))
    half_groups = pl.BlockSpec((2, 1, groups // 2, rows, width), lambda n: (0, n, 0, 0, 0))
    near_head = pl.BlockSpec((1,) + near.shape[1:], lambda n: (n, 0, 0, 0, 0, 0))
    return pl.pallas_call(
        functools.partial(finish_kernel, softmax_scale),
        grid=(kv_count,),
        out_shape=(
            jax.ShapeDtypeStruct((2, kv_count, groups // 2, rows, width), BF16),
            jax.ShapeDtypeStruct((2, kv_count, groups // 2, rows, width), BF16),
            jax.ShapeDtypeStruct(own_kv.shape, F32),
        ),
        in_specs=[
            pl.BlockSpec(memory_space=pltpu.SMEM),
            by_head,
            by_head,
            turned,
            turned,
            own,
            near_head,
            stat,
            stat,
        ],
        out_specs=(half_groups, half_groups, own),
        scratch_shapes=[pltpu.VMEM((2, 3, width, rows), BF16)],
        compiler_params=pltpu.CompilerParams(vmem_limit_bytes=GRANT),
        cost_estimate=pl.CostEstimate(
            flops=26 * kv_count * groups * rows * rows * width,
            bytes_accessed=16 * kv_count * groups * rows * width,
            transcendentals=3 * kv_count * groups * rows * rows,
        ),
        name="finish",
    )(seen, queries, grads, turned_q, turned_do, own_kv, near, lse, row_dot)


def exchange(pieces):
    return lax.ppermute(pieces, "head", [(0, 1), (1, 0)])


def spread(pieces):
    return lax.all_to_all(pieces, "ctx", split_axis=0, concat_axis=0, tiled=True)


def on_device(queries, keys, values, output_gradient, selected):
    rows_block, own_groups, kv_count, width = queries.shape
    blocks = lax.axis_size("ctx")
    own_index = lax.axis_index("ctx")
    core = lax.axis_index("head")
    half_kv = kv_count // 2
    mine, theirs = core * half_kv, (1 - core) * half_kv
    softmax_scale = width ** (-0.5)
    piece_groups = blocks // (2 * half_kv)
    piece = rows_block // piece_groups
    picks = selected.reshape(-1)
    own_picks = lax.dynamic_index_in_dim(selected, own_index, 0, keepdims=False)
    seen = (own_picks < own_index).astype(jnp.int32)

    both = jnp.stack([keys, values], axis=0)
    both = lax.dynamic_slice_in_dim(both, mine, half_kv, axis=2)
    own_kv = jnp.transpose(both, (2, 0, 1, 3))
    held = spread(own_kv.reshape(blocks, piece, width))

    inputs = jnp.transpose(jnp.stack([queries, output_gradient], axis=0), (0, 3, 2, 1, 4))
    kept = lax.dynamic_slice_in_dim(inputs, mine, half_kv, axis=1)
    fetched = exchange(lax.dynamic_slice_in_dim(inputs, theirs, half_kv, axis=1))
    inputs = jnp.concatenate([kept, fetched], axis=2)
    q_all, do_all = inputs[0], inputs[1]
    turned_q, turned_do, own_lse, own_dot = own_forward(q_all, do_all, own_kv, softmax_scale)

    near = spread(pick_pieces(held, picks))
    near = near.reshape(half_kv, 2, piece_groups, 2, piece, width)
    lse, row_dot, dnear = near_attention(
        seen, turned_q, turned_do, near, own_lse, own_dot, softmax_scale, rows_block // 2
    )
    arrived = spread(dnear.reshape(blocks, 2 * piece, width))
    kept, moved, dkv = finish(
        seen, q_all, do_all, turned_q, turned_do, own_kv, near, lse, row_dot, softmax_scale
    )
    home = spread(collect_pieces(arrived, picks))

    back = exchange(moved)
    whole = jnp.zeros((2, kv_count) + back.shape[2:], back.dtype)
    whole = lax.dynamic_update_slice_in_dim(whole, kept, mine, 1)
    whole = lax.dynamic_update_slice_in_dim(whole, back, theirs, 1)
    attn_out, grad_q = (jnp.transpose(whole[part], (2, 1, 0, 3)) for part in range(2))
    grads = (home.reshape(own_kv.shape).astype(F32) + dkv).astype(BF16)
    grad_k, grad_v = (jnp.transpose(grads[:, part], (1, 0, 2)) for part in range(2))
    return (attn_out, grad_q, grad_k, grad_v)


def solution(mesh):
    return jax.shard_map(
        on_device,
        mesh=mesh,
        in_specs=(
            P("ctx", "head", None, None),
            P("ctx", None, None),
            P("ctx", None, None),
            P("ctx", "head", None, None),
            P(),
        ),
        out_specs=(
            P("ctx", "head", None, None),
            P("ctx", "head", None, None),
            P("ctx", "head", None),
            P("ctx", "head", None),
        ),
        check_vma=False,
    )
```

time: 159 us -> 154 us (0.969)
  waiting for transfers between devices: 58.2 us -> 55.1 us
    all_to_all x4, waiting for transfers between devices: 57 us -> 53.7 us  [spread(): lax.all_to_all(pieces, 'ctx', split_axis=0, concat_axis=0, tiled=True)]
    slice x1 -> x0, local copies, waits for them, and re-layouts: 2.7 us -> none  [on_device(): back = exchange(results[:, :, own_groups:])]
  transfers between devices with their start and end apart: 6 -> 6, of which waited for: 5 -> 5; matrix products, arithmetic and copies ran while one was open for 9% -> 9% of each run, Pallas kernels for 15% -> 18%
where the time goes in v2:
time: 154 us
  waiting for transfers between devices  55.1 us (36%)
  Pallas kernels  44 us (29%)
  starting transfers between devices  36.1 us (23%)
  local copies, waits for them, and re-layouts  11.4 us (7%)
  other arithmetic  6.45 us (4%)
    all_to_all x4, waiting for transfers between devices, spread(): lax.all_to_all(pieces, 'ctx', split_axis=0, concat_axis=0, tiled=True)  53.7 us
    all_to_all x4, starting transfers between devices, spread(): lax.all_to_all(pieces, 'ctx', split_axis=0, concat_axis=0, tiled=True)  36 us
    pallas_call x1, Pallas kernels, finish(): pl.pallas_call(functools.partial(finish_kernel, softmax_scale), grid=(kv_...  16.9 us
    pallas_call x1, Pallas kernels, near_attention(): pl.pallas_call(functools.partial(near_kernel, softmax_scale, tile), grid=...  14 us
    pallas_call x1, Pallas kernels, own_forward(): pl.pallas_call(functools.partial(own_forward_kernel, softmax_scale * math...  9.05 us
  transfers between devices with their start and end apart: 6, of which 5 were waited for; matrix products, arithmetic and copies ran while one was open for 9% of the time, Pallas kernels for 18%

profile of v2, /device:TPU:32, one launch (start us, length us, event | category | flops | bytes accessed | tf_op | source)
XLA Modules:
  0.0 153.8 jit_solution(2262430834432961744)
XLA Ops:
  0.6 1.3 copy_bitcast_fusion.2
  2.8 15.0 %all-to-all-start = ((bf16[128,16,128]{2,1,0:T(8,128)(2,1)}), bf16[128,16,128]{2,1,0:T(8,128)(2,1)S(1)}, u32[]{:S(2)}, u32[]{:S(2)}) async-start(bf16[128,16,128]{2,1,0:T(8,128)(2,1)} %bitcast.9), calls=%async_computation | async-start | bytes 1048576 | tf_op jit(solution)/shard_map/all_to_all | solution.py:428
  18.1 19.8 %all-to-all-done.held = bf16[128,16,128]{2,1,0:T(8,128)(2,1)S(1)} async-done(((bf16[128,16,128]{2,1,0:T(8,128)(2,1)}), bf16[128,16,128]{2,1,0:T(8,128)(2,1)S(1)}, u32[]{:S(2)}, u32[]{:S(2)}) %all-to-all-start) | async-done | bytes 524320 | tf_op jit(solution)/shard_map/all_to_all | solution.py:428
  38.0 1.8 %pick_pieces.1 = bf16[128,32,128]{2,1,0:T(8,128)(2,1)} custom-call(s32[256]{0:T(256)S(1)} %reshape.27.picks, bf16[128,16,128]{2,1,0:T(8,128)(2,1)S(1)} %all-to-all-done.held), custom_call_target="tpu_custom_call" | custom-call | tf_op jit(solution)/shard_map/pick_pieces/pallas_call | solution.py:47
  39.8 7.7 %all-to-all-start.1 = ((bf16[128,32,128]{2,1,0:T(8,128)(2,1)}), bf16[128,32,128]{2,1,0:T(8,128)(2,1)}, u32[]{:S(2)}, u32[]{:S(2)}) async-start(bf16[128,32,128]{2,1,0:T(8,128)(2,1)} %pick_pieces.1), calls=%async_computation.1 | async-start | bytes 2097152 | tf_op jit(solution)/shard_map/all_to_all | solution.py:428
  47.5 1.6 %copy_bitcast_fusion = (bf16[1,512,2,4,128]{4,1,2,3,0:T(8,128)(2,1)S(1)}, bf16[1,512,2,4,128]{4,1,2,3,0:T(8,128)(2,1)S(1)}) fusion(bf16[512,2,4,128]{3,2,1,0:T(4,128)(2,1)S(1)} %copy-done.2, bf16[512,2,4,128]{3,2,1,0:T(4,128)(2,1)} %param.5), kind=kLoop, calls=%fused_computation.22 | loop fusion | bytes 4194304 | tf_op jit(solution)/shard_map/stack | solution.py:450
  49.1 1.2 fusion.3
  51.0 0.9 fusion.10.kv_ref
  51.9 1.4 collective-permute-done
  53.3 2.7 %fusion.6 = (bf16[2,4,512,128]{3,2,1,0:T(8,128)(2,1)}, bf16[2,4,512,128]{3,2,1,0:T(8,128)(2,1)}) fusion(bf16[2,2,2,512,128]{4,3,2,1,0:T(8,128)(2,1)} %collective-permute-done, bf16[2,2,2,512,128]{4,3,2,1,0:T(8,128)(2,1)S(1)} %get-tuple-element.37), kind=kLoop, calls=%fused_computation.15 | loop fusion | flops 1048576 | bytes 4194304 | tf_op jit(solution)/shard_map/squeeze | solution.py:454
  56.0 9.1 %own_forward.1 = (bf16[2,128,2048]{2,1,0:T(8,128)(2,1)}, bf16[2,128,2048]{2,1,0:T(8,128)(2,1)}, f32[2,8,2048]{2,1,0:T(8,128)}, f32[2,8,2048]{2,1,0:T(8,128)}) custom-call(bf16[2,4,512,128]{3,2,1,0:T(8,128)(2,1)} %get-tuple-element.35.q_ref, bf16[2,4,512,128]{3,2,1,0:T(8,128)(2,1)} %get-tuple-element.34.do_ref, bf16[2,2,512,128]{3,2,1,0:T(8,128)(2,1)} %fusion.10.kv_ref), custom_call_target="tpu_custom_call" | custom-call | flops 1073741824 | bytes 6291456 | tf_op jit(solution)/shard_map/own_forward/pallas_call | solution.py:151
  65.0 12.0 %all-to-all-done.1 = bf16[128,32,128]{2,1,0:T(8,128)(2,1)} async-done(((bf16[128,32,128]{2,1,0:T(8,128)(2,1)}), bf16[128,32,128]{2,1,0:T(8,128)(2,1)}, u32[]{:S(2)}, u32[]{:S(2)}) %all-to-all-start.1) | async-done | bytes 1048608 | tf_op jit(solution)/shard_map/all_to_all | solution.py:428
  77.0 14.0 %near_attention.1 = (f32[2,8,2048]{2,1,0:T(8,128)}, f32[2,8,2048]{2,1,0:T(8,128)}, bf16[2,2,32,2,16,128]{5,4,3,2,1,0:T(8,128)(2,1)}) custom-call(s32[2]{0:T(128)} %fusion.9.seen_ref, bf16[2,128,2048]{2,1,0:T(8,128)(2,1)} %get-tuple-element.14.qt_ref, bf16[2,128,2048]{2,1,0:T(8,128)(2,1)} %get-tuple-element.15.dot_ref, ...), custom_call_target="tpu_custom_call" | custom-call | flops 4294967296 | bytes 5242880 | tf_op jit(solution)/shard_map/near_attention/pallas_call | solution.py:274
  91.1 6.6 %all-to-all-start.2 = ((bf16[128,32,128]{2,1,0:T(8,128)(2,1)}), bf16[128,32,128]{2,1,0:T(8,128)(2,1)S(1)}, u32[]{:S(2)}, u32[]{:S(2)}) async-start(bf16[128,32,128]{2,1,0:T(8,128)(2,1)} %bitcast.41), calls=%async_computation.2 | async-start | bytes 2097152 | tf_op jit(solution)/shard_map/all_to_all | solution.py:428
  97.7 16.9 %finish.1 = (bf16[2,2,2,512,128]{4,3,2,1,0:T(8,128)(2,1)}, bf16[2,2,2,512,128]{4,3,2,1,0:T(8,128)(2,1)}, f32[2,2,512,128]{3,2,1,0:T(8,128)}) custom-call(s32[2]{0:T(128)} %fusion.9.seen_ref, bf16[2,4,512,128]{3,2,1,0:T(8,128)(2,1)} %get-tuple-element.35.q_ref, bf16[2,4,512,128]{3,2,1,0:T(8,128)(2,1)} %get-tuple-element.34.do_ref, ...), custom_call_target="tpu_custom_call" | custom-call | flops 6979321856 | bytes 8388608 | tf_op jit(solution)/shard_map/finish/pallas_call | solution.py:392
  114.7 11.1 %all-to-all-done.2.arrived = bf16[128,32,128]{2,1,0:T(8,128)(2,1)S(1)} async-done(((bf16[128,32,128]{2,1,0:T(8,128)(2,1)}), bf16[128,32,128]{2,1,0:T(8,128)(2,1)S(1)}, u32[]{:S(2)}, u32[]{:S(2)}) %all-to-all-start.2) | async-done | bytes 1048608 | tf_op jit(solution)/shard_map/all_to_all | solution.py:428
  125.8 2.2 %collect_pieces.1 = bf16[128,16,128]{2,1,0:T(8,128)(2,1)} custom-call(s32[256]{0:T(256)S(1)} %reshape.27.picks, bf16[128,32,128]{2,1,0:T(8,128)(2,1)S(1)} %all-to-all-done.2.arrived), custom_call_target="tpu_custom_call" | custom-call | tf_op jit(solution)/shard_map/collect_pieces/pallas_call | solution.py:89
  128.0 6.6 %all-to-all-start.3 = ((bf16[128,16,128]{2,1,0:T(8,128)(2,1)}), bf16[128,16,128]{2,1,0:T(8,128)(2,1)S(1)}, u32[]{:S(2)}, u32[]{:S(2)}) async-start(bf16[128,16,128]{2,1,0:T(8,128)(2,1)} %collect_pieces.1), calls=%async_computation.3 | async-start | bytes 1048576 | tf_op jit(solution)/shard_map/all_to_all | solution.py:428
  135.2 1.8 %copy_dynamic-update-slice_fusion.1 = bf16[2,4,2,512,128]{4,1,2,3,0:T(4,128)(2,1)S(1)} fusion(bf16[2,4,2,512,128]{4,1,2,3,0:T(4,128)(2,1)S(1)} %broadcast_in_dim.3, s32[]{:T(128)S(6)} %select_n.14, bf16[2,2,2,512,128]{4,3,2,1,0:T(8,128)(2,1)S(1)} %copy-done), kind=kLoop, calls=%fused_computation.21 | loop fusion | bytes 2097156 | tf_op jit(solution)/shard_map/dynamic_update_slice | solution.py:470
  137.1 1.8 %copy_dynamic-update-slice_fusion = bf16[2,4,2,512,128]{4,1,2,3,0:T(4,128)(2,1)S(1)} fusion(bf16[2,4,2,512,128]{4,1,2,3,0:T(4,128)(2,1)S(1)} %copy_dynamic-update-slice_fusion.1, s32[]{:T(128)S(6)} %select_n.15, bf16[2,2,2,512,128]{4,3,2,1,0:T(8,128)(2,1)S(1)} %collective-permute-done.1), kind=kLoop, calls=%fused_computation.20 | loop fusion | bytes 2097156 | tf_op jit(solution)/shard_map/dynamic_update_slice | solution.py:471
  138.9 2.0 %slice_bitcast_fusion = (bf16[512,2,4,128]{3,2,1,0:T(4,128)(2,1)}, bf16[512,2,4,128]{3,2,1,0:T(4,128)(2,1)}) fusion(bf16[2,4,2,512,128]{4,1,2,3,0:T(4,128)(2,1)S(1)} %copy_dynamic-update-slice_fusion), kind=kLoop, calls=%fused_computation.12 | loop fusion | bytes 4194304 | tf_op jit(solution)/shard_map/transpose | solution.py:472
  140.9 10.8 %all-to-all-done.3 = bf16[128,16,128]{2,1,0:T(8,128)(2,1)S(1)} async-done(((bf16[128,16,128]{2,1,0:T(8,128)(2,1)}), bf16[128,16,128]{2,1,0:T(8,128)(2,1)S(1)}, u32[]{:S(2)}, u32[]{:S(2)}) %all-to-all-start.3) | async-done | bytes 524320 | tf_op jit(solution)/shard_map/all_to_all | solution.py:428
  151.8 1.0 copy.24
  152.8 1.0 copy.25
  (18 shorter events, 2.7 us)
Async XLA Ops:
  0.6 17.2 %copy-start.3 = (s32[128,2]{0,1:T(2,128)S(1)}, s32[128,2]{0,1:T(2,128)}, u32[]{:S(2)}) copy-start(s32[128,2]{0,1:T(2,128)} %param.9) | copy-start | bytes 3076
  2.8 35.1 %all-to-all-start = ((bf16[128,16,128]{2,1,0:T(8,128)(2,1)}), bf16[128,16,128]{2,1,0:T(8,128)(2,1)S(1)}, u32[]{:S(2)}, u32[]{:S(2)}) async-start(bf16[128,16,128]{2,1,0:T(8,128)(2,1)} %bitcast.9), calls=%async_computation | async-start | bytes 1048576 | tf_op jit(solution)/shard_map/all_to_all | solution.py:428
  17.9 29.6 %copy-start.2 = (bf16[512,2,4,128]{3,2,1,0:T(4,128)(2,1)S(1)}, bf16[512,2,4,128]{3,2,1,0:T(4,128)(2,1)}, u32[]{:S(2)}) copy-start(bf16[512,2,4,128]{3,2,1,0:T(4,128)(2,1)} %param.8) | copy-start | bytes 3145732
  39.8 37.2 %all-to-all-start.1 = ((bf16[128,32,128]{2,1,0:T(8,128)(2,1)}), bf16[128,32,128]{2,1,0:T(8,128)(2,1)}, u32[]{:S(2)}, u32[]{:S(2)}) async-start(bf16[128,32,128]{2,1,0:T(8,128)(2,1)} %pick_pieces.1), calls=%async_computation.1 | async-start | bytes 2097152 | tf_op jit(solution)/shard_map/all_to_all | solution.py:428
  50.3 3.0 %collective-permute-start = (bf16[2,2,2,512,128]{4,3,2,1,0:T(8,128)(2,1)}, bf16[2,2,2,512,128]{4,3,2,1,0:T(8,128)(2,1)}, u32[]{:S(2)}, u32[]{:S(2)}) collective-permute-start(bf16[2,2,2,512,128]{4,3,2,1,0:T(8,128)(2,1)} %get-tuple-element.36), channel_id=1, source_target_pairs={{0,1},{1,0},{2,3},{3,2},{4,5},{5,4},{6,7},{7,6},{8,9},{9,8},{10,11... | collective-permute-start | bytes 3145736 | tf_op jit(solution)/shard_map/ppermute | solution.py:424
  91.1 34.8 %all-to-all-start.2 = ((bf16[128,32,128]{2,1,0:T(8,128)(2,1)}), bf16[128,32,128]{2,1,0:T(8,128)(2,1)S(1)}, u32[]{:S(2)}, u32[]{:S(2)}) async-start(bf16[128,32,128]{2,1,0:T(8,128)(2,1)} %bitcast.41), calls=%async_computation.2 | async-start | bytes 2097152 | tf_op jit(solution)/shard_map/all_to_all | solution.py:428
  114.6 20.6 %copy-start = (bf16[2,2,2,512,128]{4,3,2,1,0:T(8,128)(2,1)S(1)}, bf16[2,2,2,512,128]{4,3,2,1,0:T(8,128)(2,1)}, u32[]{:S(2)}) copy-start(bf16[2,2,2,512,128]{4,3,2,1,0:T(8,128)(2,1)} %get-tuple-element.20) | copy-start | bytes 3145732
  114.6 22.4 %collective-permute-start.1 = (bf16[2,2,2,512,128]{4,3,2,1,0:T(8,128)(2,1)}, bf16[2,2,2,512,128]{4,3,2,1,0:T(8,128)(2,1)S(1)}, u32[]{:S(2)}, u32[]{:S(2)}) collective-permute-start(bf16[2,2,2,512,128]{4,3,2,1,0:T(8,128)(2,1)} %get-tuple-element.21), channel_id=1, source_target_pairs={{0,1},{1,0},{2,3},{3,2},{4,5},{5,4},{6,7},{7,6},{8,9},{9,8},{10,11... | collective-permute-start | bytes 3145736 | tf_op jit(solution)/shard_map/ppermute | solution.py:424
  128.0 23.6 %all-to-all-start.3 = ((bf16[128,16,128]{2,1,0:T(8,128)(2,1)}), bf16[128,16,128]{2,1,0:T(8,128)(2,1)S(1)}, u32[]{:S(2)}, u32[]{:S(2)}) async-start(bf16[128,16,128]{2,1,0:T(8,128)(2,1)} %collect_pieces.1), calls=%async_computation.3 | async-start | bytes 1048576 | tf_op jit(solution)/shard_map/all_to_all | solution.py:428
  138.9 12.8 %copy-start.1 = (f32[2,2,512,128]{3,2,1,0:T(8,128)S(1)}, f32[2,2,512,128]{3,2,1,0:T(8,128)}, u32[]{:S(2)}) copy-start(f32[2,2,512,128]{3,2,1,0:T(8,128)} %get-tuple-element.23) | copy-start | bytes 3145732

commit v3 on v2

--- a/solution.py
+++ b/solution.py
@@ -107,7 +107,9 @@
     )
 
 
-def own_forward_kernel(log_scale, q_ref, do_ref, kv_ref, qt_ref, dot_ref, lse_ref, row_dot_ref, vt):
+def own_forward_kernel(
+    log_scale, own_groups, kept_ref, fetched_ref, kv_ref, qt_ref, dot_ref, lse_ref, row_dot_ref, vt
+):
     width = kv_ref.shape[3]
     half = kv_ref.shape[2] // 2
     seen = causal_pairs(half)
@@ -116,8 +118,9 @@
     def _():
         vt[...] = kv_ref[0, 1].T
 
-    turned_do = do_ref[0, 0].T
-    qt_ref[0] = q_ref[0, 0].T
+    here = pl.program_id(1) < own_groups
+    turned_do = jnp.where(here, kept_ref[1, 0, 0], fetched_ref[1, 0, 0]).T
+    qt_ref[0] = jnp.where(here, kept_ref[0, 0, 0], fetched_ref[0, 0, 0]).T
     dot_ref[0] = turned_do
     for tile in range(2):
         span = slice(tile * half, (tile + 1) * half)
@@ -143,13 +146,16 @@
         row_dot_ref[0, :, span] = jnp.broadcast_to(row_dot, (8, half))
 
 
-def own_forward(queries, grads, own_kv, softmax_scale):
-    kv_count, groups, rows, width = queries.shape
-    by_group = pl.BlockSpec((1, 1, rows, width), lambda n, g: (n, g, 0, 0))
+def own_forward(kept, fetched, own_kv, softmax_scale):
+    _, kv_count, own_groups, rows, width = kept.shape
+    groups = 2 * own_groups
+    one_group = (2, 1, 1, rows, width)
+    by_kept = pl.BlockSpec(one_group, lambda n, g: (0, n, jnp.minimum(g, own_groups - 1), 0, 0))
+    by_fetched = pl.BlockSpec(one_group, lambda n, g: (0, n, jnp.maximum(g - own_groups, 0), 0, 0))
     turned = pl.BlockSpec((1, width, rows), lambda n, g: (n, 0, g))
     stat = pl.BlockSpec((1, 8, rows), lambda n, g: (n, 0, g))
     return pl.pallas_call(
-        functools.partial(own_forward_kernel, softmax_scale * math.log2(math.e)),
+        functools.partial(own_forward_kernel, softmax_scale * math.log2(math.e), own_groups),
         grid=(kv_count, groups),
         out_shape=(
             jax.ShapeDtypeStruct((kv_count, width, groups * rows), BF16),
@@ -158,8 +164,8 @@
             jax.ShapeDtypeStruct((kv_count, 8, groups * rows), F32),
         ),
         in_specs=[
-            by_group,
-            by_group,
+            by_kept,
+            by_fetched,
             pl.BlockSpec((1, 2, rows, width), lambda n, g: (n, 0, 0, 0)),
         ],
         out_specs=(turned, turned, stat, stat),
@@ -171,7 +177,7 @@
             transcendentals=kv_count * groups * rows * rows,
         ),
         name="own_forward",
-    )(queries, grads, own_kv)
+    )(kept, fetched, own_kv)
 
 
 def near_kernel(
@@ -298,8 +304,8 @@
 def finish_kernel(
     softmax_scale,
     seen_ref,
-    q_ref,
-    do_ref,
+    mine_ref,
+    other_ref,
     qt_ref,
     dot_ref,
     kv_ref,
@@ -312,7 +318,8 @@
     turned_kv,
 ):
     log_scale = softmax_scale * math.log2(math.e)
-    group_count, block = q_ref.shape[1:3]
+    own_groups, block = mine_ref.shape[2:4]
+    group_count = 2 * own_groups
     groups, _, piece, width = near_ref.shape[2:]
     tile = block // 2
     triangle = causal_pairs(tile)
@@ -363,12 +370,13 @@
             sums[at, kind] = sums[at, kind] + term if (at, kind) in sums else term
         group, rows = at // 2, slice(at % 2 * tile, (at % 2 + 1) * tile)
         if j == 2:
+            rows_ref = mine_ref if group < own_groups else other_ref
             cols = slice(col * tile, (col + 1) * tile)
-            dkv_ref[0, 0, cols, :] += dot_nn(grad_scores, q_ref[0, group, rows, :])
-            dkv_ref[0, 1, cols, :] += dot_nn(low, do_ref[0, group, rows, :])
+            dkv_ref[0, 0, cols, :] += dot_nn(grad_scores, rows_ref[0, 0, group % own_groups, rows, :])
+            dkv_ref[0, 1, cols, :] += dot_nn(low, rows_ref[1, 0, group % own_groups, rows, :])
             if col == at % 2:
-                out_ref = kept_ref if 2 * group < group_count else moved_ref
-                group = group % (group_count // 2)
+                out_ref = kept_ref if group < own_groups else moved_ref
+                group = group % own_groups
                 out_ref[0, 0, group, rows, :] = sums.pop((at, 1)).astype(BF16).T
                 out_ref[1, 0, group, rows, :] = (
                     (sums.pop((at, 0)) * softmax_scale).astype(BF16).T
@@ -381,26 +389,26 @@
     dkv_ref[0, 0] = dkv_ref[0, 0] * softmax_scale
 
 
-def finish(seen, queries, grads, turned_q, turned_do, own_kv, near, lse, row_dot, softmax_scale):
-    kv_count, groups, rows, width = queries.shape
-    by_head = pl.BlockSpec((1, groups, rows, width), lambda n: (n, 0, 0, 0))
+def finish(seen, kept, fetched, turned_q, turned_do, own_kv, near, lse, row_dot, softmax_scale):
+    _, kv_count, own_groups, rows, width = kept.shape
+    groups = 2 * own_groups
     own = pl.BlockSpec((1, 2, rows, width), lambda n: (n, 0, 0, 0))
     turned = pl.BlockSpec((1, width, groups * rows), lambda n: (n, 0, 0))
     stat = pl.BlockSpec((1, 8, groups * rows), lambda n: (n, 0, 0))
-    half_groups = pl.BlockSpec((2, 1, groups // 2, rows, width), lambda n: (0, n, 0, 0, 0))
+    half_groups = pl.BlockSpec((2, 1, own_groups, rows, width), lambda n: (0, n, 0, 0, 0))
     near_head = pl.BlockSpec((1,) + near.shape[1:], lambda n: (n, 0, 0, 0, 0, 0))
     return pl.pallas_call(
         functools.partial(finish_kernel, softmax_scale),
         grid=(kv_count,),
         out_shape=(
-            jax.ShapeDtypeStruct((2, kv_count, groups // 2, rows, width), BF16),
-            jax.ShapeDtypeStruct((2, kv_count, groups // 2, rows, width), BF16),
+            jax.ShapeDtypeStruct(kept.shape, BF16),
+            jax.ShapeDtypeStruct(kept.shape, BF16),
             jax.ShapeDtypeStruct(own_kv.shape, F32),
         ),
         in_specs=[
             pl.BlockSpec(memory_space=pltpu.SMEM),
-            by_head,
-            by_head,
+            half_groups,
+            half_groups,
             turned,
             turned,
             own,
@@ -417,7 +425,7 @@
             transcendentals=3 * kv_count * groups * rows * rows,
         ),
         name="finish",
-    )(seen, queries, grads, turned_q, turned_do, own_kv, near, lse, row_dot)
+    )(seen, kept, fetched, turned_q, turned_do, own_kv, near, lse, row_dot)
 
 
 def exchange(pieces):
@@ -445,14 +453,12 @@
     both = jnp.stack([keys, values], axis=0)
     both = lax.dynamic_slice_in_dim(both, mine, half_kv, axis=2)
     own_kv = jnp.transpose(both, (2, 0, 1, 3))
-    held = spread(own_kv.reshape(blocks, piece, width))
-
     inputs = jnp.transpose(jnp.stack([queries, output_gradient], axis=0), (0, 3, 2, 1, 4))
     kept = lax.dynamic_slice_in_dim(inputs, mine, half_kv, axis=1)
     fetched = exchange(lax.dynamic_slice_in_dim(inputs, theirs, half_kv, axis=1))
-    inputs = jnp.concatenate([kept, fetched], axis=2)
-    q_all, do_all = inputs[0], inputs[1]
-    turned_q, turned_do, own_lse, own_dot = own_forward(q_all, do_all, own_kv, softmax_scale)
+
+    held = spread(own_kv.reshape(blocks, piece, width))
+    turned_q, turned_do, own_lse, own_dot = own_forward(kept, fetched, own_kv, softmax_scale)
 
     near = spread(pick_pieces(held, picks))
     near = near.reshape(half_kv, 2, piece_groups, 2, piece, width)
@@ -461,7 +467,7 @@
     )
     arrived = spread(dnear.reshape(blocks, 2 * piece, width))
     kept, moved, dkv = finish(
-        seen, q_all, do_all, turned_q, turned_do, own_kv, near, lse, row_dot, softmax_scale
+        seen, kept, fetched, turned_q, turned_do, own_kv, near, lse, row_dot, softmax_scale
     )
     home = spread(collect_pieces(arrived, picks))
 

time: 154 us -> 154 us (level)
  other arithmetic: 6.45 us -> 3.64 us
  waiting for transfers between devices: 55.1 us -> 57.8 us
    all_to_all x4, waiting for transfers between devices: 53.7 us -> 56.5 us  [spread(): lax.all_to_all(pieces, 'ctx', split_axis=0, concat_axis=0, tiled=True)]
    squeeze x1 -> x0, other arithmetic: 2.7 us -> none  [on_device(): q_all, do_all = (inputs[0], inputs[1])]
  transfers between devices with their start and end apart: 6 -> 6, of which waited for: 5 -> 5; matrix products, arithmetic and copies ran while one was open for 9% -> 7% of each run, Pallas kernels for 18% -> 18%
where the time goes in v3:
time: 154 us
  waiting for transfers between devices  57.8 us (38%)
  Pallas kernels  44.1 us (29%)
  starting transfers between devices  36.2 us (24%)
  local copies, waits for them, and re-layouts  11.4 us (7%)
  other arithmetic  3.64 us (2%)
    all_to_all x4, waiting for transfers between devices, spread(): lax.all_to_all(pieces, 'ctx', split_axis=0, concat_axis=0, tiled=True)  56.5 us
    all_to_all x4, starting transfers between devices, spread(): lax.all_to_all(pieces, 'ctx', split_axis=0, concat_axis=0, tiled=True)  36.1 us
    pallas_call x1, Pallas kernels, finish(): pl.pallas_call(functools.partial(finish_kernel, softmax_scale), grid=(kv_...  16.9 us
    pallas_call x1, Pallas kernels, near_attention(): pl.pallas_call(functools.partial(near_kernel, softmax_scale, tile), grid=...  14 us
    pallas_call x1, Pallas kernels, own_forward(): pl.pallas_call(functools.partial(own_forward_kernel, softmax_scale * math...  9.14 us
  transfers between devices with their start and end apart: 6, of which 5 were waited for; matrix products, arithmetic and copies ran while one was open for 7% of the time, Pallas kernels for 18%

profile of v3, /device:TPU:32, one launch (start us, length us, event | category | flops | bytes accessed | tf_op | source)
XLA Modules:
  0.0 153.9 jit_solution(6573433049819015054)
XLA Ops:
  0.6 1.3 copy_bitcast_fusion.2
  2.0 0.9 fusion.5
  2.8 15.0 %all-to-all-start = ((bf16[128,16,128]{2,1,0:T(8,128)(2,1)}), bf16[128,16,128]{2,1,0:T(8,128)(2,1)S(1)}, u32[]{:S(2)}, u32[]{:S(2)}) async-start(bf16[128,16,128]{2,1,0:T(8,128)(2,1)} %bitcast.7), calls=%async_computation | async-start | bytes 1048576 | tf_op jit(solution)/shard_map/all_to_all | solution.py:436
  18.1 19.8 %all-to-all-done.held = bf16[128,16,128]{2,1,0:T(8,128)(2,1)S(1)} async-done(((bf16[128,16,128]{2,1,0:T(8,128)(2,1)}), bf16[128,16,128]{2,1,0:T(8,128)(2,1)S(1)}, u32[]{:S(2)}, u32[]{:S(2)}) %all-to-all-start) | async-done | bytes 524320 | tf_op jit(solution)/shard_map/all_to_all | solution.py:436
  38.0 1.8 %pick_pieces.1 = bf16[128,32,128]{2,1,0:T(8,128)(2,1)} custom-call(s32[256]{0:T(256)S(1)} %reshape.27.picks, bf16[128,16,128]{2,1,0:T(8,128)(2,1)S(1)} %all-to-all-done.held), custom_call_target="tpu_custom_call" | custom-call | tf_op jit(solution)/shard_map/pick_pieces/pallas_call | solution.py:47
  39.8 7.7 %all-to-all-start.1 = ((bf16[128,32,128]{2,1,0:T(8,128)(2,1)}), bf16[128,32,128]{2,1,0:T(8,128)(2,1)}, u32[]{:S(2)}, u32[]{:S(2)}) async-start(bf16[128,32,128]{2,1,0:T(8,128)(2,1)} %pick_pieces.1), calls=%async_computation.1 | async-start | bytes 2097152 | tf_op jit(solution)/shard_map/all_to_all | solution.py:436
  47.5 1.6 %copy_bitcast_fusion = (bf16[1,512,2,4,128]{4,1,2,3,0:T(8,128)(2,1)S(1)}, bf16[1,512,2,4,128]{4,1,2,3,0:T(8,128)(2,1)S(1)}) fusion(bf16[512,2,4,128]{3,2,1,0:T(4,128)(2,1)S(1)} %copy-done.2, bf16[512,2,4,128]{3,2,1,0:T(4,128)(2,1)} %param.5), kind=kLoop, calls=%fused_computation.16 | loop fusion | bytes 4194304 | tf_op jit(solution)/shard_map/stack | solution.py:456
  49.1 1.2 fusion.1
  50.9 0.8 fusion.7.kv_ref
  51.8 1.3 collective-permute-done.fetched_ref.other_ref
  53.0 9.1 %own_forward.1 = (bf16[2,128,2048]{2,1,0:T(8,128)(2,1)}, bf16[2,128,2048]{2,1,0:T(8,128)(2,1)}, f32[2,8,2048]{2,1,0:T(8,128)}, f32[2,8,2048]{2,1,0:T(8,128)}) custom-call(bf16[2,2,2,512,128]{4,3,2,1,0:T(8,128)(2,1)} %get-tuple-element.35.kept_ref.mine_ref, bf16[2,2,2,512,128]{4,3,2,1,0:T(8,128)(2,1)} %collective-permute-done.fetched_ref.other_ref, ...), custom_call_target="tpu_custom_call" | custom-call | flops 1073741824 | bytes 6291456 | tf_op jit(solution)/shard_map/own_forward/pallas_call | solution.py:157
  62.2 14.8 %all-to-all-done.1 = bf16[128,32,128]{2,1,0:T(8,128)(2,1)} async-done(((bf16[128,32,128]{2,1,0:T(8,128)(2,1)}), bf16[128,32,128]{2,1,0:T(8,128)(2,1)}, u32[]{:S(2)}, u32[]{:S(2)}) %all-to-all-start.1) | async-done | bytes 1048608 | tf_op jit(solution)/shard_map/all_to_all | solution.py:436
  77.0 14.0 %near_attention.1 = (f32[2,8,2048]{2,1,0:T(8,128)}, f32[2,8,2048]{2,1,0:T(8,128)}, bf16[2,2,32,2,16,128]{5,4,3,2,1,0:T(8,128)(2,1)}) custom-call(s32[2]{0:T(128)} %fusion.6.seen_ref, bf16[2,128,2048]{2,1,0:T(8,128)(2,1)} %get-tuple-element.14.qt_ref, bf16[2,128,2048]{2,1,0:T(8,128)(2,1)} %get-tuple-element.15.dot_ref, ...), custom_call_target="tpu_custom_call" | custom-call | flops 4294967296 | bytes 5242880 | tf_op jit(solution)/shard_map/near_attention/pallas_call | solution.py:280
  91.0 6.8 %all-to-all-start.2 = ((bf16[128,32,128]{2,1,0:T(8,128)(2,1)}), bf16[128,32,128]{2,1,0:T(8,128)(2,1)S(1)}, u32[]{:S(2)}, u32[]{:S(2)}) async-start(bf16[128,32,128]{2,1,0:T(8,128)(2,1)} %bitcast.37), calls=%async_computation.2 | async-start | bytes 2097152 | tf_op jit(solution)/shard_map/all_to_all | solution.py:436
  97.8 16.9 %finish.1 = (bf16[2,2,2,512,128]{4,3,2,1,0:T(8,128)(2,1)}, bf16[2,2,2,512,128]{4,3,2,1,0:T(8,128)(2,1)}, f32[2,2,512,128]{3,2,1,0:T(8,128)}) custom-call(s32[2]{0:T(128)} %fusion.6.seen_ref, bf16[2,2,2,512,128]{4,3,2,1,0:T(8,128)(2,1)} %get-tuple-element.35.kept_ref.mine_ref, bf16[2,2,2,512,128]{4,3,2,1,0:T(8,128)(2,1)} %collective-permute-done.fetched_ref.other_ref, ...), custom_call_target="tpu_custom_call" | custom-call | flops 6979321856 | bytes 8388608 | tf_op jit(solution)/shard_map/finish/pallas_call | solution.py:400
  114.9 11.1 %all-to-all-done.2.arrived = bf16[128,32,128]{2,1,0:T(8,128)(2,1)S(1)} async-done(((bf16[128,32,128]{2,1,0:T(8,128)(2,1)}), bf16[128,32,128]{2,1,0:T(8,128)(2,1)S(1)}, u32[]{:S(2)}, u32[]{:S(2)}) %all-to-all-start.2) | async-done | bytes 1048608 | tf_op jit(solution)/shard_map/all_to_all | solution.py:436
  126.0 2.3 %collect_pieces.1 = bf16[128,16,128]{2,1,0:T(8,128)(2,1)} custom-call(s32[256]{0:T(256)S(1)} %reshape.27.picks, bf16[128,32,128]{2,1,0:T(8,128)(2,1)S(1)} %all-to-all-done.2.arrived), custom_call_target="tpu_custom_call" | custom-call | tf_op jit(solution)/shard_map/collect_pieces/pallas_call | solution.py:89
  128.2 6.6 %all-to-all-start.3 = ((bf16[128,16,128]{2,1,0:T(8,128)(2,1)}), bf16[128,16,128]{2,1,0:T(8,128)(2,1)S(1)}, u32[]{:S(2)}, u32[]{:S(2)}) async-start(bf16[128,16,128]{2,1,0:T(8,128)(2,1)} %collect_pieces.1), calls=%async_computation.3 | async-start | bytes 1048576 | tf_op jit(solution)/shard_map/all_to_all | solution.py:436
  135.4 1.8 %copy_dynamic-update-slice_fusion.1 = bf16[2,4,2,512,128]{4,1,2,3,0:T(4,128)(2,1)S(1)} fusion(bf16[2,4,2,512,128]{4,1,2,3,0:T(4,128)(2,1)S(1)} %broadcast_in_dim.3, s32[]{:T(128)S(6)} %select_n.14, bf16[2,2,2,512,128]{4,3,2,1,0:T(8,128)(2,1)S(1)} %copy-done), kind=kLoop, calls=%fused_computation.15 | loop fusion | bytes 2097156 | tf_op jit(solution)/shard_map/dynamic_update_slice | solution.py:476
  137.2 1.8 %copy_dynamic-update-slice_fusion = bf16[2,4,2,512,128]{4,1,2,3,0:T(4,128)(2,1)S(1)} fusion(bf16[2,4,2,512,128]{4,1,2,3,0:T(4,128)(2,1)S(1)} %copy_dynamic-update-slice_fusion.1, s32[]{:T(128)S(6)} %select_n.15, bf16[2,2,2,512,128]{4,3,2,1,0:T(8,128)(2,1)S(1)} %collective-permute-done.1), kind=kLoop, calls=%fused_computation.14 | loop fusion | bytes 2097156 | tf_op jit(solution)/shard_map/dynamic_update_slice | solution.py:477
  139.1 2.0 %slice_bitcast_fusion = (bf16[512,2,4,128]{3,2,1,0:T(4,128)(2,1)}, bf16[512,2,4,128]{3,2,1,0:T(4,128)(2,1)}) fusion(bf16[2,4,2,512,128]{4,1,2,3,0:T(4,128)(2,1)S(1)} %copy_dynamic-update-slice_fusion), kind=kLoop, calls=%fused_computation.8 | loop fusion | bytes 4194304 | tf_op jit(solution)/shard_map/transpose | solution.py:478
  141.1 10.8 %all-to-all-done.3 = bf16[128,16,128]{2,1,0:T(8,128)(2,1)S(1)} async-done(((bf16[128,16,128]{2,1,0:T(8,128)(2,1)}), bf16[128,16,128]{2,1,0:T(8,128)(2,1)S(1)}, u32[]{:S(2)}, u32[]{:S(2)}) %all-to-all-start.3) | async-done | bytes 524320 | tf_op jit(solution)/shard_map/all_to_all | solution.py:436
  152.0 1.0 copy.24
  153.0 1.0 copy.25
  (17 shorter events, 1.7 us)
Async XLA Ops:
  0.6 17.2 %copy-start.3 = (s32[128,2]{0,1:T(2,128)S(1)}, s32[128,2]{0,1:T(2,128)}, u32[]{:S(2)}) copy-start(s32[128,2]{0,1:T(2,128)} %param.9) | copy-start | bytes 3076
  2.8 35.1 %all-to-all-start = ((bf16[128,16,128]{2,1,0:T(8,128)(2,1)}), bf16[128,16,128]{2,1,0:T(8,128)(2,1)S(1)}, u32[]{:S(2)}, u32[]{:S(2)}) async-start(bf16[128,16,128]{2,1,0:T(8,128)(2,1)} %bitcast.7), calls=%async_computation | async-start | bytes 1048576 | tf_op jit(solution)/shard_map/all_to_all | solution.py:436
  17.9 29.6 %copy-start.2 = (bf16[512,2,4,128]{3,2,1,0:T(4,128)(2,1)S(1)}, bf16[512,2,4,128]{3,2,1,0:T(4,128)(2,1)}, u32[]{:S(2)}) copy-start(bf16[512,2,4,128]{3,2,1,0:T(4,128)(2,1)} %param.8) | copy-start | bytes 3145732
  39.8 37.2 %all-to-all-start.1 = ((bf16[128,32,128]{2,1,0:T(8,128)(2,1)}), bf16[128,32,128]{2,1,0:T(8,128)(2,1)}, u32[]{:S(2)}, u32[]{:S(2)}) async-start(bf16[128,32,128]{2,1,0:T(8,128)(2,1)} %pick_pieces.1), calls=%async_computation.1 | async-start | bytes 2097152 | tf_op jit(solution)/shard_map/all_to_all | solution.py:436
  50.3 2.8 %collective-permute-start = (bf16[2,2,2,512,128]{4,3,2,1,0:T(8,128)(2,1)S(1)}, bf16[2,2,2,512,128]{4,3,2,1,0:T(8,128)(2,1)}, u32[]{:S(2)}, u32[]{:S(2)}) collective-permute-start(bf16[2,2,2,512,128]{4,3,2,1,0:T(8,128)(2,1)S(1)} %get-tuple-element.34), channel_id=1, source_target_pairs={{0,1},{1,0},{2,3},{3,2},{4,5},{5,4},{6,7},{7,6},{8,9},{9,8},{10,11... | collective-permute-start | bytes 3145736 | tf_op jit(solution)/shard_map/ppermute | solution.py:432
  91.0 35.0 %all-to-all-start.2 = ((bf16[128,32,128]{2,1,0:T(8,128)(2,1)}), bf16[128,32,128]{2,1,0:T(8,128)(2,1)S(1)}, u32[]{:S(2)}, u32[]{:S(2)}) async-start(bf16[128,32,128]{2,1,0:T(8,128)(2,1)} %bitcast.37), calls=%async_computation.2 | async-start | bytes 2097152 | tf_op jit(solution)/shard_map/all_to_all | solution.py:436
  114.8 20.6 %copy-start = (bf16[2,2,2,512,128]{4,3,2,1,0:T(8,128)(2,1)S(1)}, bf16[2,2,2,512,128]{4,3,2,1,0:T(8,128)(2,1)}, u32[]{:S(2)}) copy-start(bf16[2,2,2,512,128]{4,3,2,1,0:T(8,128)(2,1)} %get-tuple-element.20) | copy-start | bytes 3145732
  114.8 22.5 %collective-permute-start.1 = (bf16[2,2,2,512,128]{4,3,2,1,0:T(8,128)(2,1)}, bf16[2,2,2,512,128]{4,3,2,1,0:T(8,128)(2,1)S(1)}, u32[]{:S(2)}, u32[]{:S(2)}) collective-permute-start(bf16[2,2,2,512,128]{4,3,2,1,0:T(8,128)(2,1)} %get-tuple-element.21), channel_id=1, source_target_pairs={{0,1},{1,0},{2,3},{3,2},{4,5},{5,4},{6,7},{7,6},{8,9},{9,8},{10,11... | collective-permute-start | bytes 3145736 | tf_op jit(solution)/shard_map/ppermute | solution.py:432
  128.2 23.6 %all-to-all-start.3 = ((bf16[128,16,128]{2,1,0:T(8,128)(2,1)}), bf16[128,16,128]{2,1,0:T(8,128)(2,1)S(1)}, u32[]{:S(2)}, u32[]{:S(2)}) async-start(bf16[128,16,128]{2,1,0:T(8,128)(2,1)} %collect_pieces.1), calls=%async_computation.3 | async-start | bytes 1048576 | tf_op jit(solution)/shard_map/all_to_all | solution.py:436
  139.0 12.8 %copy-start.1 = (f32[2,2,512,128]{3,2,1,0:T(8,128)S(1)}, f32[2,2,512,128]{3,2,1,0:T(8,128)}, u32[]{:S(2)}) copy-start(f32[2,2,512,128]{3,2,1,0:T(8,128)} %get-tuple-element.23) | copy-start | bytes 3145732

commit v4 on v2

--- a/solution.py
+++ b/solution.py
@@ -470,8 +470,14 @@
     whole = lax.dynamic_update_slice_in_dim(whole, kept, mine, 1)
     whole = lax.dynamic_update_slice_in_dim(whole, back, theirs, 1)
     attn_out, grad_q = (jnp.transpose(whole[part], (2, 1, 0, 3)) for part in range(2))
-    grads = (home.reshape(own_kv.shape).astype(F32) + dkv).astype(BF16)
-    grad_k, grad_v = (jnp.transpose(grads[:, part], (1, 0, 2)) for part in range(2))
+    home = home.reshape(own_kv.shape)
+    grad_k, grad_v = (
+        (
+            jnp.stack([home[n, part] for n in range(half_kv)], axis=1).astype(F32)
+            + jnp.stack([dkv[n, part] for n in range(half_kv)], axis=1)
+        ).astype(BF16)
+        for part in range(2)
+    )
     return (attn_out, grad_q, grad_k, grad_v)
 
 

time: 154 us -> 154 us (level)
  no operation moved by 1% of the time
where the time goes in v4:
time: 154 us
  waiting for transfers between devices  54.3 us (35%)
  Pallas kernels  44 us (29%)
  starting transfers between devices  36.1 us (23%)
  local copies, waits for them, and re-layouts  12.2 us (8%)
  other arithmetic  6.39 us (4%)
    all_to_all x4, waiting for transfers between devices, spread(): lax.all_to_all(pieces, 'ctx', split_axis=0, concat_axis=0, tiled=True)  52.9 us
    all_to_all x4, starting transfers between devices, spread(): lax.all_to_all(pieces, 'ctx', split_axis=0, concat_axis=0, tiled=True)  36 us
    pallas_call x1, Pallas kernels, finish(): pl.pallas_call(functools.partial(finish_kernel, softmax_scale), grid=(kv_...  16.9 us
    pallas_call x1, Pallas kernels, near_attention(): pl.pallas_call(functools.partial(near_kernel, softmax_scale, tile), grid=...  14 us
    pallas_call x1, Pallas kernels, own_forward(): pl.pallas_call(functools.partial(own_forward_kernel, softmax_scale * math...  9.05 us
  transfers between devices with their start and end apart: 6, of which 5 were waited for; matrix products, arithmetic and copies ran while one was open for 9% of the time, Pallas kernels for 18%

profile of v4, /device:TPU:32, one launch (start us, length us, event | category | flops | bytes accessed | tf_op | source)
XLA Modules:
  0.0 153.7 jit_solution(844018029002822529)
XLA Ops:
  0.6 1.3 copy_bitcast_fusion.2
  2.0 0.9 fusion.7
  2.8 15.0 %all-to-all-start = ((bf16[128,16,128]{2,1,0:T(8,128)(2,1)}), bf16[128,16,128]{2,1,0:T(8,128)(2,1)S(1)}, u32[]{:S(2)}, u32[]{:S(2)}) async-start(bf16[128,16,128]{2,1,0:T(8,128)(2,1)} %bitcast.9), calls=%async_computation | async-start | bytes 1048576 | tf_op jit(solution)/shard_map/all_to_all | solution.py:428
  18.1 19.8 %all-to-all-done.held = bf16[128,16,128]{2,1,0:T(8,128)(2,1)S(1)} async-done(((bf16[128,16,128]{2,1,0:T(8,128)(2,1)}), bf16[128,16,128]{2,1,0:T(8,128)(2,1)S(1)}, u32[]{:S(2)}, u32[]{:S(2)}) %all-to-all-start) | async-done | bytes 524320 | tf_op jit(solution)/shard_map/all_to_all | solution.py:428
  38.0 1.8 %pick_pieces.1 = bf16[128,32,128]{2,1,0:T(8,128)(2,1)} custom-call(s32[256]{0:T(256)S(1)} %reshape.27.picks, bf16[128,16,128]{2,1,0:T(8,128)(2,1)S(1)} %all-to-all-done.held), custom_call_target="tpu_custom_call" | custom-call | tf_op jit(solution)/shard_map/pick_pieces/pallas_call | solution.py:47
  39.8 7.7 %all-to-all-start.1 = ((bf16[128,32,128]{2,1,0:T(8,128)(2,1)}), bf16[128,32,128]{2,1,0:T(8,128)(2,1)}, u32[]{:S(2)}, u32[]{:S(2)}) async-start(bf16[128,32,128]{2,1,0:T(8,128)(2,1)} %pick_pieces.1), calls=%async_computation.1 | async-start | bytes 2097152 | tf_op jit(solution)/shard_map/all_to_all | solution.py:428
  47.5 1.6 %copy_bitcast_fusion = (bf16[1,512,2,4,128]{4,1,2,3,0:T(8,128)(2,1)S(1)}, bf16[1,512,2,4,128]{4,1,2,3,0:T(8,128)(2,1)S(1)}) fusion(bf16[512,2,4,128]{3,2,1,0:T(4,128)(2,1)S(1)} %copy-done.2, bf16[512,2,4,128]{3,2,1,0:T(4,128)(2,1)} %param.5), kind=kLoop, calls=%fused_computation.20 | loop fusion | bytes 4194304 | tf_op jit(solution)/shard_map/stack | solution.py:450
  49.1 1.2 fusion.3
  51.8 1.4 collective-permute-done
  53.3 2.7 %fusion.6 = (bf16[2,4,512,128]{3,2,1,0:T(8,128)(2,1)}, bf16[2,4,512,128]{3,2,1,0:T(8,128)(2,1)}) fusion(bf16[2,2,2,512,128]{4,3,2,1,0:T(8,128)(2,1)} %collective-permute-done, bf16[2,2,2,512,128]{4,3,2,1,0:T(8,128)(2,1)S(1)} %get-tuple-element.37), kind=kLoop, calls=%fused_computation.15 | loop fusion | flops 1048576 | bytes 4194304 | tf_op jit(solution)/shard_map/squeeze | solution.py:454
  56.0 9.1 %own_forward.1 = (bf16[2,128,2048]{2,1,0:T(8,128)(2,1)}, bf16[2,128,2048]{2,1,0:T(8,128)(2,1)}, f32[2,8,2048]{2,1,0:T(8,128)}, f32[2,8,2048]{2,1,0:T(8,128)}) custom-call(bf16[2,4,512,128]{3,2,1,0:T(8,128)(2,1)} %get-tuple-element.35.q_ref, bf16[2,4,512,128]{3,2,1,0:T(8,128)(2,1)} %get-tuple-element.34.do_ref, bf16[2,2,512,128]{3,2,1,0:T(8,128)(2,1)} %fusion.11.kv_ref), custom_call_target="tpu_custom_call" | custom-call | flops 1073741824 | bytes 6291456 | tf_op jit(solution)/shard_map/own_forward/pallas_call | solution.py:151
  65.0 12.0 %all-to-all-done.1 = bf16[128,32,128]{2,1,0:T(8,128)(2,1)} async-done(((bf16[128,32,128]{2,1,0:T(8,128)(2,1)}), bf16[128,32,128]{2,1,0:T(8,128)(2,1)}, u32[]{:S(2)}, u32[]{:S(2)}) %all-to-all-start.1) | async-done | bytes 1048608 | tf_op jit(solution)/shard_map/all_to_all | solution.py:428
  77.0 14.0 %near_attention.1 = (f32[2,8,2048]{2,1,0:T(8,128)}, f32[2,8,2048]{2,1,0:T(8,128)}, bf16[2,2,32,2,16,128]{5,4,3,2,1,0:T(8,128)(2,1)}) custom-call(s32[2]{0:T(128)} %fusion.10.seen_ref, bf16[2,128,2048]{2,1,0:T(8,128)(2,1)} %get-tuple-element.14.qt_ref, bf16[2,128,2048]{2,1,0:T(8,128)(2,1)} %get-tuple-element.15.dot_ref, ...), custom_call_target="tpu_custom_call" | custom-call | flops 4294967296 | bytes 5242880 | tf_op jit(solution)/shard_map/near_attention/pallas_call | solution.py:274
  91.0 6.6 %all-to-all-start.2 = ((bf16[128,32,128]{2,1,0:T(8,128)(2,1)}), bf16[128,32,128]{2,1,0:T(8,128)(2,1)S(1)}, u32[]{:S(2)}, u32[]{:S(2)}) async-start(bf16[128,32,128]{2,1,0:T(8,128)(2,1)} %bitcast.48), calls=%async_computation.2 | async-start | bytes 2097152 | tf_op jit(solution)/shard_map/all_to_all | solution.py:428
  97.7 16.9 %finish.1 = (bf16[2,2,2,512,128]{4,3,2,1,0:T(8,128)(2,1)}, bf16[2,2,2,512,128]{4,3,2,1,0:T(8,128)(2,1)}, f32[2,2,512,128]{3,2,1,0:T(8,128)}) custom-call(s32[2]{0:T(128)} %fusion.10.seen_ref, bf16[2,4,512,128]{3,2,1,0:T(8,128)(2,1)} %get-tuple-element.35.q_ref, bf16[2,4,512,128]{3,2,1,0:T(8,128)(2,1)} %get-tuple-element.34.do_ref, ...), custom_call_target="tpu_custom_call" | custom-call | flops 6979321856 | bytes 8388608 | tf_op jit(solution)/shard_map/finish/pallas_call | solution.py:392
  114.7 11.1 %all-to-all-done.2.arrived = bf16[128,32,128]{2,1,0:T(8,128)(2,1)S(1)} async-done(((bf16[128,32,128]{2,1,0:T(8,128)(2,1)}), bf16[128,32,128]{2,1,0:T(8,128)(2,1)S(1)}, u32[]{:S(2)}, u32[]{:S(2)}) %all-to-all-start.2) | async-done | bytes 1048608 | tf_op jit(solution)/shard_map/all_to_all | solution.py:428
  125.8 2.2 %collect_pieces.1 = bf16[128,16,128]{2,1,0:T(8,128)(2,1)} custom-call(s32[256]{0:T(256)S(1)} %reshape.27.picks, bf16[128,32,128]{2,1,0:T(8,128)(2,1)S(1)} %all-to-all-done.2.arrived), custom_call_target="tpu_custom_call" | custom-call | tf_op jit(solution)/shard_map/collect_pieces/pallas_call | solution.py:89
  128.0 6.6 %all-to-all-start.3 = ((bf16[128,16,128]{2,1,0:T(8,128)(2,1)}), bf16[128,16,128]{2,1,0:T(8,128)(2,1)S(1)}, u32[]{:S(2)}, u32[]{:S(2)}) async-start(bf16[128,16,128]{2,1,0:T(8,128)(2,1)} %collect_pieces.1), calls=%async_computation.3 | async-start | bytes 1048576 | tf_op jit(solution)/shard_map/all_to_all | solution.py:428
  136.0 1.8 %copy_dynamic-update-slice_fusion.1 = bf16[2,4,2,512,128]{4,1,2,3,0:T(4,128)(2,1)S(1)} fusion(bf16[2,4,2,512,128]{4,1,2,3,0:T(4,128)(2,1)S(1)} %broadcast_in_dim.3, s32[]{:T(128)S(6)} %select_n.14, bf16[2,2,2,512,128]{4,3,2,1,0:T(8,128)(2,1)S(1)} %copy-done), kind=kLoop, calls=%fused_computation.19 | loop fusion | bytes 2097156 | tf_op jit(solution)/shard_map/dynamic_update_slice | solution.py:470
  137.8 1.8 %copy_dynamic-update-slice_fusion = bf16[2,4,2,512,128]{4,1,2,3,0:T(4,128)(2,1)S(1)} fusion(bf16[2,4,2,512,128]{4,1,2,3,0:T(4,128)(2,1)S(1)} %copy_dynamic-update-slice_fusion.1, s32[]{:T(128)S(6)} %select_n.15, bf16[2,2,2,512,128]{4,3,2,1,0:T(8,128)(2,1)S(1)} %collective-permute-done.1), kind=kLoop, calls=%fused_computation.18 | loop fusion | bytes 2097156 | tf_op jit(solution)/shard_map/dynamic_update_slice | solution.py:471
  139.6 2.0 %slice_bitcast_fusion = (bf16[512,2,4,128]{3,2,1,0:T(4,128)(2,1)}, bf16[512,2,4,128]{3,2,1,0:T(4,128)(2,1)}) fusion(bf16[2,4,2,512,128]{4,1,2,3,0:T(4,128)(2,1)S(1)} %copy_dynamic-update-slice_fusion), kind=kLoop, calls=%fused_computation.12 | loop fusion | bytes 4194304 | tf_op jit(solution)/shard_map/transpose | solution.py:472
  141.7 9.9 %all-to-all-done.3 = bf16[128,16,128]{2,1,0:T(8,128)(2,1)S(1)} async-done(((bf16[128,16,128]{2,1,0:T(8,128)(2,1)}), bf16[128,16,128]{2,1,0:T(8,128)(2,1)S(1)}, u32[]{:S(2)}, u32[]{:S(2)}) %all-to-all-start.3) | async-done | bytes 524320 | tf_op jit(solution)/shard_map/all_to_all | solution.py:428
  151.7 1.0 copy.25
  152.8 1.0 copy.24
  (22 shorter events, 3.4 us)
Async XLA Ops:
  0.6 17.2 %copy-start.4 = (s32[128,2]{0,1:T(2,128)S(1)}, s32[128,2]{0,1:T(2,128)}, u32[]{:S(2)}) copy-start(s32[128,2]{0,1:T(2,128)} %param.9) | copy-start | bytes 3076
  2.8 35.1 %all-to-all-start = ((bf16[128,16,128]{2,1,0:T(8,128)(2,1)}), bf16[128,16,128]{2,1,0:T(8,128)(2,1)S(1)}, u32[]{:S(2)}, u32[]{:S(2)}) async-start(bf16[128,16,128]{2,1,0:T(8,128)(2,1)} %bitcast.9), calls=%async_computation | async-start | bytes 1048576 | tf_op jit(solution)/shard_map/all_to_all | solution.py:428
  17.9 29.6 %copy-start.2 = (bf16[512,2,4,128]{3,2,1,0:T(4,128)(2,1)S(1)}, bf16[512,2,4,128]{3,2,1,0:T(4,128)(2,1)}, u32[]{:S(2)}) copy-start(bf16[512,2,4,128]{3,2,1,0:T(4,128)(2,1)} %param.8) | copy-start | bytes 3145732
  39.8 37.2 %all-to-all-start.1 = ((bf16[128,32,128]{2,1,0:T(8,128)(2,1)}), bf16[128,32,128]{2,1,0:T(8,128)(2,1)}, u32[]{:S(2)}, u32[]{:S(2)}) async-start(bf16[128,32,128]{2,1,0:T(8,128)(2,1)} %pick_pieces.1), calls=%async_computation.1 | async-start | bytes 2097152 | tf_op jit(solution)/shard_map/all_to_all | solution.py:428
  50.2 3.0 %collective-permute-start = (bf16[2,2,2,512,128]{4,3,2,1,0:T(8,128)(2,1)}, bf16[2,2,2,512,128]{4,3,2,1,0:T(8,128)(2,1)}, u32[]{:S(2)}, u32[]{:S(2)}) collective-permute-start(bf16[2,2,2,512,128]{4,3,2,1,0:T(8,128)(2,1)} %get-tuple-element.36), channel_id=1, source_target_pairs={{0,1},{1,0},{2,3},{3,2},{4,5},{5,4},{6,7},{7,6},{8,9},{9,8},{10,11... | collective-permute-start | bytes 3145736 | tf_op jit(solution)/shard_map/ppermute | solution.py:424
  91.0 34.8 %all-to-all-start.2 = ((bf16[128,32,128]{2,1,0:T(8,128)(2,1)}), bf16[128,32,128]{2,1,0:T(8,128)(2,1)S(1)}, u32[]{:S(2)}, u32[]{:S(2)}) async-start(bf16[128,32,128]{2,1,0:T(8,128)(2,1)} %bitcast.48), calls=%async_computation.2 | async-start | bytes 2097152 | tf_op jit(solution)/shard_map/all_to_all | solution.py:428
  114.6 20.1 %copy-start.1 = (f32[2,2,512,128]{3,2,1,0:T(8,128)S(1)}, f32[2,2,512,128]{3,2,1,0:T(8,128)}, u32[]{:S(2)}) copy-start(f32[2,2,512,128]{3,2,1,0:T(8,128)} %get-tuple-element.23) | copy-start | bytes 3145732
  114.6 23.2 %collective-permute-start.1 = (bf16[2,2,2,512,128]{4,3,2,1,0:T(8,128)(2,1)}, bf16[2,2,2,512,128]{4,3,2,1,0:T(8,128)(2,1)S(1)}, u32[]{:S(2)}, u32[]{:S(2)}) collective-permute-start(bf16[2,2,2,512,128]{4,3,2,1,0:T(8,128)(2,1)} %get-tuple-element.21), channel_id=1, source_target_pairs={{0,1},{1,0},{2,3},{3,2},{4,5},{5,4},{6,7},{7,6},{8,9},{9,8},{10,11... | collective-permute-start | bytes 3145736 | tf_op jit(solution)/shard_map/ppermute | solution.py:424
  128.0 23.6 %all-to-all-start.3 = ((bf16[128,16,128]{2,1,0:T(8,128)(2,1)}), bf16[128,16,128]{2,1,0:T(8,128)(2,1)S(1)}, u32[]{:S(2)}, u32[]{:S(2)}) async-start(bf16[128,16,128]{2,1,0:T(8,128)(2,1)} %collect_pieces.1), calls=%async_computation.3 | async-start | bytes 1048576 | tf_op jit(solution)/shard_map/all_to_all | solution.py:428
  134.7 1.3 copy-start
  139.6 12.0 %copy-start.3 = (f32[512,1,128]{2,0,1:T(8,128)S(1)}, f32[512,1,128]{2,0,1:T(8,128)}, u32[]{:S(2)}) copy-start(f32[512,1,128]{2,0,1:T(8,128)} %get-tuple-element.39) | copy-start | bytes 786436
